TPU v7x, 128 devices: a whole 4x4x4 slice. The times are simulated.
128 devices in a mesh: src: 8 (over y, core), tgt: 16 (over x, z).
Axes of the slice: x: 4, y: 4, z: 4, core: 2. Of those that a mesh axis runs over, the one named last changes fastest.
Arguments:
- sources: float32 [256, 16384], P('tgt', 'src'), may hold values from -24 to 24, as said below
- targets: float32 [256, 16384], P('src', 'tgt'), may hold values from -24 to 24, as said below
- source_logw: float32 [16384], P('src'), may hold values from -1 to 1
- target_logw: float32 [16384], P('tgt'), may hold values from -1 to 1
- times: float32 [16384], P('src'), may hold values from 0 to 1
Outputs:
- row_potential: float32 [16384], P('src')
- moved: float32 [256, 16384], P('tgt', 'src')
- col_potential: float32 [16384], P('tgt')
Inputs may be any that keep to these rules, and one draw needn't show every extreme that they name: `sources`: point coordinates. `targets`: point coordinates.
All inputs are finite; a program needn't handle non-finite values.
Results may differ from a plain program's by a relative error of at most 0.00025.
Values sent between devices are 32-bit elements; how exact they have to be, the bound alone decides.
A program may use at most 64 MiB of HBM per device.

v0:
```python
import jax
import jax.numpy as jnp
from jax import lax
from jax.sharding import Mesh
from jax.sharding import PartitionSpec as P

ITERS = 2
TGT = ("tgt_0", "tgt_1")


EPSILON = 16.0


def from_everyone(shard, axis):
    copies = jnp.broadcast_to(shard, (lax.axis_size(axis), *shard.shape))
    return lax.all_to_all(copies, axis, split_axis=0, concat_axis=0, tiled=True)


def collected_together(shard, axis):
    leaves = jax.tree.leaves(shard)
    sequence = sorted(range(len(leaves)), key=lambda k: -leaves[k].size)
    width = (1, *leaves[sequence[0]].shape)[-1]
    lines = [
        jnp.pad(leaves[k].reshape(-1), (0, -leaves[k].size % width)).reshape(-1, width)
        for k in sequence
    ]
    both, at, found = (from_everyone(jnp.concatenate(lines), axis), 0, {})
    for k, line in zip(sequence, lines):
        piece = both[:, at : at + len(line)].reshape(len(both), -1)
        found[k] = piece[:, : leaves[k].size].reshape(-1, *leaves[k].shape)
        at += len(line)
    numbers = iter(range(len(leaves)))
    return jax.tree.map(lambda _: found[next(numbers)], shard)


def collected_alike(shard, axis):
    leaves, found = (jax.tree.leaves(shard), {})
    for leading, a in enumerate(leaves):
        if leading not in found:
            alike = [k for k, b in enumerate(leaves) if b.dtype == a.dtype]
            got = (
                collected_together([leaves[k] for k in alike], axis)
                if len(alike) > 1
                else [from_everyone(a, axis)]
            )
            for k, b in zip(alike, got):
                found[k] = b
    numbers = iter(range(len(leaves)))
    return jax.tree.map(lambda _: found[next(numbers)], shard)


def joined_by_halves(pieces, combine):
    while len(jax.tree.leaves(pieces)[0]) > 1:
        pieces = jax.vmap(combine)(
            *(jax.tree.map(lambda part: part[side::2], pieces) for side in (0, 1))
        )
    return jax.tree.map(lambda part: part[0], pieces)


def merged(shard, axis, combine):
    pieces = collected_alike(shard, axis)
    return joined_by_halves(pieces, combine)


def combined_all(shard, axis, combine):
    pieces = collected_together(shard, axis)
    return joined_by_halves(pieces, combine)


def gather_axes(shard, axes, dim):
    if not axes:
        return shard
    nearer = lax.all_gather(shard, axes[-1], axis=dim, tiled=True)
    return gather_axes(nearer, axes[:-1], dim)


def in_order(pieces, dim):
    pieces = jnp.moveaxis(pieces, 0, dim)
    dims = pieces.shape
    return pieces.reshape(*dims[:dim], dims[dim] * dims[dim + 1], *dims[dim + 2 :])


def gathered_copies(shard, axis, dim):
    return in_order(from_everyone(shard, axis), dim)


def split_up(shard, dim, length):
    dims = shard.shape
    pieces = shard.reshape(*dims[:dim], length, dims[dim] // length, *dims[dim + 1 :])
    return jnp.moveaxis(pieces, dim, 0)


def sum_at_owner(shard, axis, dim):
    pieces = split_up(shard, dim, lax.axis_size(axis))
    arrived = lax.all_to_all(pieces, axis, split_axis=0, concat_axis=0, tiled=True)
    return arrived.sum(axis=0)


def by_axis(shard, axes):
    for axis in axes:
        shard = lax.psum(shard, axis)
    return shard


def cost_block(rows, cols):
    cross = jnp.dot(
        rows, cols.T, precision=lax.Precision.HIGHEST, preferred_element_type=jnp.float32
    )
    return 0.5 * jnp.sum(rows * rows, 1)[:, None] + 0.5 * jnp.sum(cols * cols, 1)[None, :] - cross


def combine_lse(first, second):
    top = jnp.maximum(first[0], second[0])
    return (top, first[1] * jnp.exp(first[0] - top) + second[1] * jnp.exp(second[0] - top))


def merge_rows(top, total):
    top, total = merged((top, total), TGT, combine_lse)
    return top + jnp.log(total)


def merge_cols(top, total):
    top, total = combined_all((top, total), "src", combine_lse)
    return top + jnp.log(total)


def row_partials(blocks, cols_full, col_pot):

    def one(blk):
        scores = (col_pot[None, :] - cost_block(blk, cols_full)) / EPSILON
        top = jnp.max(scores, 1)
        return (top, jnp.sum(jnp.exp(scores - top[:, None]), 1))

    top, total = lax.map(one, blocks)
    return (top.reshape(-1), total.reshape(-1))


def col_partials(blocks, cols_full, row_pot):
    count, block = (blocks.shape[0], blocks.shape[1])
    cols = cols_full.shape[0]

    def step(carry, item):
        top, total = carry
        blk, pot = item
        scores = (pot[:, None] - cost_block(blk, cols_full)) / EPSILON
        fresh = jnp.maximum(top, jnp.max(scores, 0))
        total = total * jnp.exp(top - fresh) + jnp.sum(jnp.exp(scores - fresh[None, :]), 0)
        return ((fresh, total), None)

    init = (jnp.full((cols,), -1e30, jnp.float32), jnp.zeros((cols,), jnp.float32))
    (top, total), _ = lax.scan(step, init, (blocks, row_pot.reshape(count, block)))
    return (top, total)


def per_device(sources, targets, source_logw, target_logw, times):
    rows_full = gather_axes(sources, TGT, 0).T
    cols_full = gathered_copies(targets, "src", 0).T
    rows = rows_full.shape[0]
    width = rows_full.shape[1]
    block = min(512, rows)
    count = rows // block
    blocks = rows_full.reshape(count, block, width)
    col_pot = jnp.zeros((cols_full.shape[0],), jnp.float32)
    row_pot = jnp.zeros((rows,), jnp.float32)
    for sweep in range(ITERS):
        top, total = row_partials(blocks, cols_full, col_pot)
        row_pot = EPSILON * (source_logw - merge_rows(top, total))
        top, total = col_partials(blocks, cols_full, row_pot)
        col_pot = EPSILON * (target_logw - merge_cols(top, total))

    def transport(item):
        blk, pot = item
        plan = jnp.exp((pot[:, None] + col_pot[None, :] - cost_block(blk, cols_full)) / EPSILON)
        weighted = jnp.dot(
            plan, cols_full, precision=lax.Precision.HIGHEST, preferred_element_type=jnp.float32
        )
        return (weighted, jnp.sum(plan, 1))

    weighted, mass = lax.map(transport, (blocks, row_pot.reshape(count, block)))
    weighted = weighted.reshape(rows, width)
    mass = mass.reshape(rows)
    share = sum_at_owner(weighted.T, TGT, 0)
    mass = by_axis(mass, TGT)
    moved = (1.0 - times)[None, :] * sources + times[None, :] * (share / mass[None, :])
    moved_full = gathered_copies(moved, TGT, 0).T
    top, total = col_partials(moved_full.reshape(count, block, width), cols_full, row_pot)
    final_pot = EPSILON * (target_logw - merge_cols(top, total))
    return (row_pot, moved, final_pot)


def solution(mesh):
    torus = Mesh(mesh.devices.reshape(mesh.shape["src"], 4, 4), ("src", "tgt_0", "tgt_1"))
    placed = (P(TGT, "src"), P("src", TGT), P("src"), P(TGT), P("src"))
    return jax.shard_map(
        per_device,
        mesh=torus,
        in_specs=placed,
        out_specs=(P("src"), P(TGT, "src"), P(TGT)),
        check_vma=False,
    )
```

profile of v0, /device:TPU:1, one launch (start us, length us, event | category | flops | bytes accessed | tf_op | source)
XLA Modules:
  0.0 319.8 jit_solution(11078589268936942676)
XLA Ops:
  7.2 14.3 %all_gather.6 = f32[64,2048]{1,0:T(8,128)} all-gather(f32[16,2048]{1,0:T(8,128)} %param.17), channel_id=1, replica_groups=mesh['src'=8,'tgt_0'=4,'tgt_1'=4] {'tgt_1'}, dimensions={0}, use_global_device_ids=true | all-gather | bytes 655360 | tf_op jit(solution)/shard_map/all_gather | solution.py:73
  23.6 7.7 %all-to-all-start = ((f32[8,32,1024]{2,1,0:T(8,128)}), f32[8,32,1024]{2,1,0:T(8,128)S(1)}, u32[]{:S(2)}, u32[]{:S(2)}) async-start(f32[8,32,1024]{2,1,0:T(8,128)} %broadcast_in_dim.82), calls=%async_computation | async-start | bytes 2097152 | tf_op jit(solution)/shard_map/all_to_all | solution.py:16
  31.3 15.1 %all-to-all-done = f32[8,32,1024]{2,1,0:T(8,128)S(1)} async-done(((f32[8,32,1024]{2,1,0:T(8,128)}), f32[8,32,1024]{2,1,0:T(8,128)S(1)}, u32[]{:S(2)}, u32[]{:S(2)}) %all-to-all-start) | async-done | bytes 1048608 | tf_op jit(solution)/shard_map/all_to_all | solution.py:16
  46.5 8.6 %all-gather.2.cloned.1.call-done = f32[256,2048]{1,0:T(8,128)} async-done(((f32[64,2048]{1,0:T(8,128)}), f32[256,2048]{1,0:T(8,128)}) %all-gather.2.cloned.1.call-update) | async-done | bytes 2097168 | tf_op jit(solution)/shard_map/all_gather | solution.py:73
  57.1 12.1 %while.87 = (s32[]{:T(128)}, f32[4,512]{1,0:T(4,128)S(1)}, f32[4,512]{1,0:T(4,128)S(1)}, f32[4,512,256]{2,1,0:T(8,128)S(1)}, f32[1024]{0:T(1024)S(1)}, /*index=5*/f32[256,1024]{1,0:T(8,128)S(1)}, s32[]{:T(128)}, s32[]{:T(128)}) while((s32[]{:T(128)}, f32[4,512]{1,0:T(4,128)S(1)}, f32[4,512]{1,0:T(4,128)S(1)}, f32[4,512,256]{2,1,0:T(8,128)S(1)}, ...), condition=%wide.region_5.6_spmd, body=%wide.region_1.5_spmd.sunk | while | flops 1614544896 | bytes 6326373 | solution.py:134
  70.0 5.4 %all-to-all-start.1 = ((f32[16,2,2048]{2,1,0:T(2,128)}), f32[16,2,2048]{2,1,0:T(2,128)S(1)}, u32[]{:S(2)}, u32[]{:S(2)}) async-start(f32[16,2,2048]{2,1,0:T(2,128)} %broadcast_in_dim.83), calls=%async_computation.1 | async-start | bytes 524288 | tf_op jit(solution)/shard_map/all_to_all | solution.py:16
  75.5 7.4 %all-to-all-done.1 = f32[16,2,2048]{2,1,0:T(2,128)S(1)} async-done(((f32[16,2,2048]{2,1,0:T(2,128)}), f32[16,2,2048]{2,1,0:T(2,128)S(1)}, u32[]{:S(2)}, u32[]{:S(2)}) %all-to-all-start.1) | async-done | bytes 262176 | tf_op jit(solution)/shard_map/all_to_all | solution.py:16
  84.5 22.4 %while.90 = (s32[]{:T(128)}, f32[1024]{0:T(1024)S(1)}, f32[1024]{0:T(1024)S(1)}, f32[4,512]{1,0:T(4,128)S(1)}, f32[4,512,256]{2,1,0:T(8,128)S(1)}, /*index=5*/f3...) while((s32[]{:T(128)}, f32[1024]{0:T(1024)S(1)}, f32[1024]{0:T(1024)S(1)}, ...), condition=%wide.region_10.11_spmd.clone, body=%wide.region_6.10_spmd.clone.sunk | while | flops 1614551040 | bytes 6371444 | solution.py:151
  84.7 3.5 %fusion.95 = (f32[1024]{0:T(1024)S(1)}, f32[512,1024]{1,0:T(8,128)}) fusion(f32[256,1024]{1,0:T(8,128)S(1)} %get-tuple-element.1096, f32[4,512,256]{2,1,0:T(8,128)S(1)} %get-tuple-element.1094, s32[]{:T(128)} %get-tuple-element.1081, f32[1024]{0:T(1024)S(1)} %broadcast_multiply_fusion.30, f32[512]{0:T(512)S(1)} %broadcast_multiply_fusion.31, ...), kind=kOutput, calls=%fused_computation.136.clone.1 | convolution fusion | flops 1613233152 | bytes 3682308 | tf_op jit(solution)/shard_map/while/body/eval_jaxpr/dot_general | solution.py:106
  90.3 3.5 %fusion.95 = (f32[1024]{0:T(1024)S(1)}, f32[512,1024]{1,0:T(8,128)}) fusion(f32[256,1024]{1,0:T(8,128)S(1)} %get-tuple-element.1096, f32[4,512,256]{2,1,0:T(8,128)S(1)} %get-tuple-element.1094, s32[]{:T(128)} %get-tuple-element.1081, f32[1024]{0:T(1024)S(1)} %broadcast_multiply_fusion.30, f32[512]{0:T(512)S(1)} %broadcast_multiply_fusion.31, ...), kind=kOutput, calls=%fused_computation.136.clone.1 | convolution fusion | flops 1613233152 | bytes 3682308 | tf_op jit(solution)/shard_map/while/body/eval_jaxpr/dot_general | solution.py:106
  95.9 3.5 %fusion.95 = (f32[1024]{0:T(1024)S(1)}, f32[512,1024]{1,0:T(8,128)}) fusion(f32[256,1024]{1,0:T(8,128)S(1)} %get-tuple-element.1096, f32[4,512,256]{2,1,0:T(8,128)S(1)} %get-tuple-element.1094, s32[]{:T(128)} %get-tuple-element.1081, f32[1024]{0:T(1024)S(1)} %broadcast_multiply_fusion.30, f32[512]{0:T(512)S(1)} %broadcast_multiply_fusion.31, ...), kind=kOutput, calls=%fused_computation.136.clone.1 | convolution fusion | flops 1613233152 | bytes 3682308 | tf_op jit(solution)/shard_map/while/body/eval_jaxpr/dot_general | solution.py:106
  101.5 3.5 %fusion.95 = (f32[1024]{0:T(1024)S(1)}, f32[512,1024]{1,0:T(8,128)}) fusion(f32[256,1024]{1,0:T(8,128)S(1)} %get-tuple-element.1096, f32[4,512,256]{2,1,0:T(8,128)S(1)} %get-tuple-element.1094, s32[]{:T(128)} %get-tuple-element.1081, f32[1024]{0:T(1024)S(1)} %broadcast_multiply_fusion.30, f32[512]{0:T(512)S(1)} %broadcast_multiply_fusion.31, ...), kind=kOutput, calls=%fused_computation.136.clone.1 | convolution fusion | flops 1613233152 | bytes 3682308 | tf_op jit(solution)/shard_map/while/body/eval_jaxpr/dot_general | solution.py:106
  107.6 6.3 %all-to-all-start.2 = ((f32[8,2,1024]{2,1,0:T(2,128)}), f32[8,2,1024]{2,1,0:T(2,128)S(1)}, u32[]{:S(2)}, u32[]{:S(2)}) async-start(f32[8,2,1024]{2,1,0:T(2,128)} %broadcast_in_dim.84), calls=%async_computation.2 | async-start | bytes 131072 | tf_op jit(solution)/shard_map/all_to_all | solution.py:16
  113.9 4.9 %all-to-all-done.2 = f32[8,2,1024]{2,1,0:T(2,128)S(1)} async-done(((f32[8,2,1024]{2,1,0:T(2,128)}), f32[8,2,1024]{2,1,0:T(2,128)S(1)}, u32[]{:S(2)}, u32[]{:S(2)}) %all-to-all-start.2) | async-done | bytes 65568 | tf_op jit(solution)/shard_map/all_to_all | solution.py:16
  119.2 12.1 %while.88 = (s32[]{:T(128)}, f32[4,512]{1,0:T(4,128)S(1)}, f32[4,512]{1,0:T(4,128)S(1)}, f32[1024]{0:T(1024)S(1)}, f32[4,512,256]{2,1,0:T(8,128)S(1)}, /*index=5...) while((s32[]{:T(128)}, f32[4,512]{1,0:T(4,128)S(1)}, f32[4,512]{1,0:T(4,128)S(1)}, ...), condition=%wide.region_15.16_spmd, body=%wide.region_11.15_spmd.sunk | while | flops 1614544896 | bytes 6330477 | solution.py:134
  119.4 2.2 fusion.86
  125.4 2.2 fusion.86
  128.5 2.2 fusion.86
  132.2 3.7 %all-to-all-start.3 = ((f32[16,2,2048]{2,1,0:T(2,128)}), f32[16,2,2048]{2,1,0:T(2,128)S(1)}, u32[]{:S(2)}, u32[]{:S(2)}) async-start(f32[16,2,2048]{2,1,0:T(2,128)} %broadcast_in_dim.85), calls=%async_computation.3 | async-start | bytes 524288 | tf_op jit(solution)/shard_map/all_to_all | solution.py:16
  135.9 7.3 %all-to-all-done.3 = f32[16,2,2048]{2,1,0:T(2,128)S(1)} async-done(((f32[16,2,2048]{2,1,0:T(2,128)}), f32[16,2,2048]{2,1,0:T(2,128)S(1)}, u32[]{:S(2)}, u32[]{:S(2)}) %all-to-all-start.3) | async-done | bytes 262176 | tf_op jit(solution)/shard_map/all_to_all | solution.py:16
  145.3 22.4 %while.91 = (s32[]{:T(128)}, f32[1024]{0:T(1024)S(1)}, f32[1024]{0:T(1024)S(1)}, f32[4,512]{1,0:T(4,128)S(1)}, f32[4,512,256]{2,1,0:T(8,128)S(1)}, /*index=5*/f3...) while((s32[]{:T(128)}, f32[1024]{0:T(1024)S(1)}, f32[1024]{0:T(1024)S(1)}, ...), condition=%wide.region_20.21_spmd.clone, body=%wide.region_16.20_spmd.clone.sunk | while | flops 1614551040 | bytes 6371444 | solution.py:151
  145.5 3.5 %fusion.99 = (f32[1024]{0:T(1024)S(1)}, f32[512,1024]{1,0:T(8,128)}) fusion(f32[256,1024]{1,0:T(8,128)S(1)} %get-tuple-element.1150, f32[4,512,256]{2,1,0:T(8,128)S(1)} %get-tuple-element.1148, s32[]{:T(128)} %get-tuple-element.1135, f32[1024]{0:T(1024)S(1)} %broadcast_multiply_fusion.32, f32[512]{0:T(512)S(1)} %broadcast_multiply_fusion.33, ...), kind=kOutput, calls=%fused_computation.137.clone.1 | convolution fusion | flops 1613233152 | bytes 3682308 | tf_op jit(solution)/shard_map/while/body/eval_jaxpr/dot_general | solution.py:106
  151.1 3.5 %fusion.99 = (f32[1024]{0:T(1024)S(1)}, f32[512,1024]{1,0:T(8,128)}) fusion(f32[256,1024]{1,0:T(8,128)S(1)} %get-tuple-element.1150, f32[4,512,256]{2,1,0:T(8,128)S(1)} %get-tuple-element.1148, s32[]{:T(128)} %get-tuple-element.1135, f32[1024]{0:T(1024)S(1)} %broadcast_multiply_fusion.32, f32[512]{0:T(512)S(1)} %broadcast_multiply_fusion.33, ...), kind=kOutput, calls=%fused_computation.137.clone.1 | convolution fusion | flops 1613233152 | bytes 3682308 | tf_op jit(solution)/shard_map/while/body/eval_jaxpr/dot_general | solution.py:106
  156.8 3.5 %fusion.99 = (f32[1024]{0:T(1024)S(1)}, f32[512,1024]{1,0:T(8,128)}) fusion(f32[256,1024]{1,0:T(8,128)S(1)} %get-tuple-element.1150, f32[4,512,256]{2,1,0:T(8,128)S(1)} %get-tuple-element.1148, s32[]{:T(128)} %get-tuple-element.1135, f32[1024]{0:T(1024)S(1)} %broadcast_multiply_fusion.32, f32[512]{0:T(512)S(1)} %broadcast_multiply_fusion.33, ...), kind=kOutput, calls=%fused_computation.137.clone.1 | convolution fusion | flops 1613233152 | bytes 3682308 | tf_op jit(solution)/shard_map/while/body/eval_jaxpr/dot_general | solution.py:106
  162.4 3.5 %fusion.99 = (f32[1024]{0:T(1024)S(1)}, f32[512,1024]{1,0:T(8,128)}) fusion(f32[256,1024]{1,0:T(8,128)S(1)} %get-tuple-element.1150, f32[4,512,256]{2,1,0:T(8,128)S(1)} %get-tuple-element.1148, s32[]{:T(128)} %get-tuple-element.1135, f32[1024]{0:T(1024)S(1)} %broadcast_multiply_fusion.32, f32[512]{0:T(512)S(1)} %broadcast_multiply_fusion.33, ...), kind=kOutput, calls=%fused_computation.137.clone.1 | convolution fusion | flops 1613233152 | bytes 3682308 | tf_op jit(solution)/shard_map/while/body/eval_jaxpr/dot_general | solution.py:106
  168.5 5.2 %all-to-all-start.4 = ((f32[8,2,1024]{2,1,0:T(2,128)}), f32[8,2,1024]{2,1,0:T(2,128)S(1)}, u32[]{:S(2)}, u32[]{:S(2)}) async-start(f32[8,2,1024]{2,1,0:T(2,128)} %broadcast_in_dim.87), calls=%async_computation.4 | async-start | bytes 131072 | tf_op jit(solution)/shard_map/all_to_all | solution.py:16
  175.3 3.3 %all-to-all-done.4 = f32[8,2,1024]{2,1,0:T(2,128)S(1)} async-done(((f32[8,2,1024]{2,1,0:T(2,128)}), f32[8,2,1024]{2,1,0:T(2,128)S(1)}, u32[]{:S(2)}, u32[]{:S(2)}) %all-to-all-start.4) | async-done | bytes 65568 | tf_op jit(solution)/shard_map/all_to_all | solution.py:16
  179.0 26.2 %while.89 = (s32[]{:T(128)}, f32[4,512,256]{2,1,0:T(8,128)}, f32[4,512]{1,0:T(4,128)S(1)}, f32[4,512]{1,0:T(4,128)S(1)}, f32[1024]{0:T(1024)S(1)}, /*index=5*/f3...) while((s32[]{:T(128)}, f32[4,512,256]{2,1,0:T(8,128)}, ...), condition=%wide.region_24.25_spmd, body=%wide.region_21.24_spmd.sunk | while | flops 3224633856 | bytes 7901821 | solution.py:179
  179.2 3.7 %fusion.91 = (f32[512]{0:T(512)S(1)}, f32[512,1024]{1,0:T(8,128)S(1)}) fusion(f32[256,1024]{1,0:T(8,128)} %get-tuple-element.1182, f32[4,512,256]{2,1,0:T(8,128)S(1)} %get-tuple-element.1180, s32[]{:T(128)} %get-tuple-element.1164, f32[1024]{0:T(1024)S(1)} %broadcast_multiply_fusion.28, f32[512]{0:T(512)S(1)} %broadcast_multiply_fusion.29, ...), kind=kOutput, calls=%fused_computation.135.clone.1 | convolution fusion | flops 1613757952 | bytes 3684356 | tf_op jit(solution)/shard_map/while/body/eval_jaxpr/dot_general | solution.py:106
  182.9 2.6 fusion.92
  185.8 3.7 %fusion.91 = (f32[512]{0:T(512)S(1)}, f32[512,1024]{1,0:T(8,128)S(1)}) fusion(f32[256,1024]{1,0:T(8,128)} %get-tuple-element.1182, f32[4,512,256]{2,1,0:T(8,128)S(1)} %get-tuple-element.1180, s32[]{:T(128)} %get-tuple-element.1164, f32[1024]{0:T(1024)S(1)} %broadcast_multiply_fusion.28, f32[512]{0:T(512)S(1)} %broadcast_multiply_fusion.29, ...), kind=kOutput, calls=%fused_computation.135.clone.1 | convolution fusion | flops 1613757952 | bytes 3684356 | tf_op jit(solution)/shard_map/while/body/eval_jaxpr/dot_general | solution.py:106
  189.4 2.6 fusion.92
  192.3 3.7 %fusion.91 = (f32[512]{0:T(512)S(1)}, f32[512,1024]{1,0:T(8,128)S(1)}) fusion(f32[256,1024]{1,0:T(8,128)} %get-tuple-element.1182, f32[4,512,256]{2,1,0:T(8,128)S(1)} %get-tuple-element.1180, s32[]{:T(128)} %get-tuple-element.1164, f32[1024]{0:T(1024)S(1)} %broadcast_multiply_fusion.28, f32[512]{0:T(512)S(1)} %broadcast_multiply_fusion.29, ...), kind=kOutput, calls=%fused_computation.135.clone.1 | convolution fusion | flops 1613757952 | bytes 3684356 | tf_op jit(solution)/shard_map/while/body/eval_jaxpr/dot_general | solution.py:106
  196.0 2.6 fusion.92
  198.9 3.7 %fusion.91 = (f32[512]{0:T(512)S(1)}, f32[512,1024]{1,0:T(8,128)S(1)}) fusion(f32[256,1024]{1,0:T(8,128)} %get-tuple-element.1182, f32[4,512,256]{2,1,0:T(8,128)S(1)} %get-tuple-element.1180, s32[]{:T(128)} %get-tuple-element.1164, f32[1024]{0:T(1024)S(1)} %broadcast_multiply_fusion.28, f32[512]{0:T(512)S(1)} %broadcast_multiply_fusion.29, ...), kind=kOutput, calls=%fused_computation.135.clone.1 | convolution fusion | flops 1613757952 | bytes 3684356 | tf_op jit(solution)/shard_map/while/body/eval_jaxpr/dot_general | solution.py:106
  202.5 2.6 fusion.92
  205.2 2.9 copy.25
  208.1 3.8 %all-to-all-start.5 = ((f32[16,16,2048]{2,1,0:T(8,128)}), f32[16,16,2048]{2,1,0:T(8,128)S(1)}, u32[]{:S(2)}, u32[]{:S(2)}) async-start(f32[16,16,2048]{2,1,0:T(8,128)} %bitcast.199), calls=%async_computation.5 | async-start | bytes 4194304 | tf_op jit(solution)/shard_map/all_to_all | solution.py:95
  212.0 27.9 %psum.14 = f32[2048]{0:T(1024)S(1)} all-reduce(f32[2048]{0:T(1024)S(1)} %bitcast.241), channel_id=1, replica_groups=mesh['src'=8,'tgt_0'=4,'tgt_1'=4] {'tgt_0'}, use_global_device_ids=true, to_apply=%region_26.27 | all-reduce | flops 2048 | bytes 16384 | tf_op jit(solution)/shard_map/psum | solution.py:101
  239.9 8.2 %psum.15 = f32[2048]{0:T(1024)S(1)} all-reduce(f32[2048]{0:T(1024)S(1)} %psum.14), channel_id=1, replica_groups=mesh['src'=8,'tgt_0'=4,'tgt_1'=4] {'tgt_1'}, use_global_device_ids=true, to_apply=%region_27.28 | all-reduce | flops 2048 | bytes 16384 | tf_op jit(solution)/shard_map/psum | solution.py:101
  249.8 3.9 %all-to-all-start.6 = ((f32[16,16,2048]{2,1,0:T(8,128)}), f32[16,16,2048]{2,1,0:T(8,128)S(1)}, u32[]{:S(2)}, u32[]{:S(2)}) async-start(f32[16,16,2048]{2,1,0:T(8,128)} %broadcast_in_dim.88), calls=%async_computation.6 | async-start | bytes 4194304 | tf_op jit(solution)/shard_map/all_to_all | solution.py:16
  253.8 23.0 %all-to-all-done.6 = f32[16,16,2048]{2,1,0:T(8,128)S(1)} async-done(((f32[16,16,2048]{2,1,0:T(8,128)}), f32[16,16,2048]{2,1,0:T(8,128)S(1)}, u32[]{:S(2)}, u32[]{:S(2)}) %all-to-all-start.6) | async-done | bytes 2097184 | tf_op jit(solution)/shard_map/all_to_all | solution.py:16
  278.7 19.1 %while.92 = (s32[]{:T(128)}, f32[1024]{0:T(1024)S(1)}, f32[1024]{0:T(1024)S(1)}, f32[4,512]{1,0:T(4,128)S(1)}, f32[4,512,256]{2,1,0:T(8,128)}, /*index=5*/f32[10...) while((s32[]{:T(128)}, f32[1024]{0:T(1024)S(1)}, f32[1024]{0:T(1024)S(1)}, ...), condition=%wide.region_32.33_spmd.clone, body=%wide.region_28.32_spmd.clone.sunk | while | flops 1614551040 | bytes 6371952 | solution.py:151
  279.9 3.2 fusion.103
  284.7 3.2 fusion.103
  289.4 3.2 fusion.103
  294.2 3.2 fusion.103
  297.8 14.2 %all_to_all.40 = f32[8,2,1024]{2,1,0:T(2,128)S(1)} all-to-all(f32[8,2,1024]{2,1,0:T(2,128)S(1)} %broadcast_in_dim.89), channel_id=1, replica_groups=mesh['src'=8,'tgt_0'=4,'tgt_1'=4] {'src'}, dimensions={0} | all-to-all | bytes 131072 | tf_op jit(solution)/shard_map/all_to_all | solution.py:16
  (308 shorter events, 58.6 us)
Async XLA Ops:
  7.2 48.0 %all-gather.2.cloned.1.call-start = ((), (), s32[]{:S(2)}) async-start(), calls=%async_computation.8 | async-start | bytes 2621440 | tf_op jit(solution)/shard_map/all_gather | solution.py:73
  23.6 22.8 %all-to-all-start = ((f32[8,32,1024]{2,1,0:T(8,128)}), f32[8,32,1024]{2,1,0:T(8,128)S(1)}, u32[]{:S(2)}, u32[]{:S(2)}) async-start(f32[8,32,1024]{2,1,0:T(8,128)} %broadcast_in_dim.82), calls=%async_computation | async-start | bytes 2097152 | tf_op jit(solution)/shard_map/all_to_all | solution.py:16
  70.0 12.9 %all-to-all-start.1 = ((f32[16,2,2048]{2,1,0:T(2,128)}), f32[16,2,2048]{2,1,0:T(2,128)S(1)}, u32[]{:S(2)}, u32[]{:S(2)}) async-start(f32[16,2,2048]{2,1,0:T(2,128)} %broadcast_in_dim.83), calls=%async_computation.1 | async-start | bytes 524288 | tf_op jit(solution)/shard_map/all_to_all | solution.py:16
  84.5 34.7 %copy-start.4 = (f32[1024]{0:T(1024)S(1)}, f32[1024]{0:T(1024)}, u32[]{:S(2)}) copy-start(f32[1024]{0:T(1024)} %param.20) | copy-start | bytes 12292
  107.6 11.1 %all-to-all-start.2 = ((f32[8,2,1024]{2,1,0:T(2,128)}), f32[8,2,1024]{2,1,0:T(2,128)S(1)}, u32[]{:S(2)}, u32[]{:S(2)}) async-start(f32[8,2,1024]{2,1,0:T(2,128)} %broadcast_in_dim.84), calls=%async_computation.2 | async-start | bytes 131072 | tf_op jit(solution)/shard_map/all_to_all | solution.py:16
  132.2 11.0 %all-to-all-start.3 = ((f32[16,2,2048]{2,1,0:T(2,128)}), f32[16,2,2048]{2,1,0:T(2,128)S(1)}, u32[]{:S(2)}, u32[]{:S(2)}) async-start(f32[16,2,2048]{2,1,0:T(2,128)} %broadcast_in_dim.85), calls=%async_computation.3 | async-start | bytes 524288 | tf_op jit(solution)/shard_map/all_to_all | solution.py:16
  144.7 0.6 copy-start.6
  167.8 6.0 %copy-start = (f32[256,1024]{1,0:T(8,128)}, f32[256,1024]{1,0:T(8,128)S(1)}, u32[]{:S(2)}) copy-start(f32[256,1024]{1,0:T(8,128)S(1)} %get-tuple-element.1222) | copy-start | bytes 3145732
  168.5 10.1 %all-to-all-start.4 = ((f32[8,2,1024]{2,1,0:T(2,128)}), f32[8,2,1024]{2,1,0:T(2,128)S(1)}, u32[]{:S(2)}, u32[]{:S(2)}) async-start(f32[8,2,1024]{2,1,0:T(2,128)} %broadcast_in_dim.87), calls=%async_computation.4 | async-start | bytes 131072 | tf_op jit(solution)/shard_map/all_to_all | solution.py:16
  208.1 3.9 %copy-start.5 = (f32[2048]{0:T(1024)S(1)}, f32[2048]{0:T(1024)}, u32[]{:S(2)}) copy-start(f32[2048]{0:T(1024)} %param.21) | copy-start | bytes 24580
  208.1 39.9 %all-to-all-start.5 = ((f32[16,16,2048]{2,1,0:T(8,128)}), f32[16,16,2048]{2,1,0:T(8,128)S(1)}, u32[]{:S(2)}, u32[]{:S(2)}) async-start(f32[16,16,2048]{2,1,0:T(8,128)} %bitcast.199), calls=%async_computation.5 | async-start | bytes 4194304 | tf_op jit(solution)/shard_map/all_to_all | solution.py:95
  212.0 36.2 %copy-start.2 = (f32[16,2048]{1,0:T(8,128)S(1)}, f32[16,2048]{1,0:T(8,128)}, u32[]{:S(2)}) copy-start(f32[16,2048]{1,0:T(8,128)} %param.17) | copy-start | bytes 393220
  248.2 1.6 copy-start.3
  249.8 26.9 %all-to-all-start.6 = ((f32[16,16,2048]{2,1,0:T(8,128)}), f32[16,16,2048]{2,1,0:T(8,128)S(1)}, u32[]{:S(2)}, u32[]{:S(2)}) async-start(f32[16,16,2048]{2,1,0:T(8,128)} %broadcast_in_dim.88), calls=%async_computation.6 | async-start | bytes 4194304 | tf_op jit(solution)/shard_map/all_to_all | solution.py:16
  276.8 1.9 copy-start.1
Sparse Core Ops, SparseCore 0:
  21.7 33.4 all-gather.1
where the time goes:
time: 322 us; the launch traced here: 320 us
  matrix products  83.3 us (26%)
  waiting for transfers between devices  69.6 us (22%)
  blocking collectives  64.5 us (20%)
  starting transfers between devices  36.2 us (11%)
  other arithmetic  31.7 us (10%)
  local copies, waits for them, and re-layouts  18.7 us (6%)
  between operations  14.7 us (5%)
    dot_general x24, matrix products, cost_block(): jnp.dot(rows, cols.T, precision=lax.Precision.HIGHEST, preferred_element_...  72.8 us
    all_to_all x6, waiting for transfers between devices, from_everyone(): return lax.all_to_all(copies, axis, split_axis=0, concat_axis=0, tiled=True)  60.9 us
    psum x2, blocking collectives, by_axis(): shard = lax.psum(shard, axis)  36 us
    all_to_all x6, starting transfers between devices, from_everyone(): return lax.all_to_all(copies, axis, split_axis=0, concat_axis=0, tiled=True)  32.3 us
    reduce_sum x12, other arithmetic, step(): jnp.sum(jnp.exp(scores - fresh[None, :]), 0)  16.6 us
    all_gather x1, blocking collectives, gather_axes(): nearer = lax.all_gather(shard, axes[-1], axis=dim, tiled=True)  14.3 us
    all_to_all x1, blocking collectives, from_everyone(): return lax.all_to_all(copies, axis, split_axis=0, concat_axis=0, tiled=True)  14.2 us
    dot_general x4, matrix products, transport(): jnp.dot(plan, cols_full, precision=lax.Precision.HIGHEST, preferred_eleme...  10.5 us
  transfers between devices with their start and end apart: 8, of which 7 were waited for; matrix products, arithmetic and copies ran while one was open for 1% of the time, Pallas kernels for 0%

commit v1 on v0

v1 whole, which is shorter than its diff:
```python
import functools

import jax
import jax.numpy as jnp
from jax import lax
from jax.experimental import pallas as pl
from jax.experimental.pallas import tpu as pltpu
from jax.sharding import PartitionSpec as P

MESH = pl.DeviceIdType.MESH
F32 = jnp.float32
BF16 = jnp.bfloat16
EPSILON = 16.0
LOG2E = 1.4426950408889634
LN2 = 0.6931471805599453
SCALE = LOG2E / EPSILON

FEATURES = 256
ROWS = 2048
COLS = 1024
SIDE = 4
PLANE = 16
LINE = 8
COPIES = 240


def halves(a):
    high = a.astype(BF16)
    return high, (a - high.astype(F32)).astype(BF16)


def kernel(
    src, tgt, slw, tlw, tim,
    rowp, moved, colp,
    sg, tg, mg, tcat, scat, q, e, w, tw, eh, el,
    r1, r2, q1, q2, vr, vc, nb, sb, cb, lrow, frow, phi,
    send_sem, recv_sem,
):
    me_s, me_t = lax.axis_index("src"), lax.axis_index("tgt")
    x, z = me_t // SIDE, me_t % SIDE
    y, core = me_s // 2, me_s % 2
    started = []

    def send(source, target, device):
        k = len(started)
        copy = pltpu.make_async_remote_copy(
            src_ref=source, dst_ref=target, send_sem=send_sem.at[k], recv_sem=recv_sem.at[k],
            device_id=device, device_id_type=MESH,
        )
        copy.start()
        started.append(copy)
        return copy

    def wrap(value):
        return lax.rem(value + SIDE, SIDE)

    def tgt_at(dx, dz):
        return wrap(x + dx) * SIDE + wrap(z + dz)

    def plane_dev(dx, dz):
        return (me_s, tgt_at(dx, dz))

    def at(h, first, second):
        return (first, second) if h == 0 else (second, first)

    barrier = pltpu.get_barrier_semaphore()
    for k in range(1, PLANE):
        pl.semaphore_signal(barrier, inc=1, device_id=(me_s, lax.rem(me_t + k, PLANE)), device_id_type=MESH)
    for k in range(1, LINE):
        pl.semaphore_signal(barrier, inc=1, device_id=(lax.rem(me_s + k, LINE), me_t), device_id_type=MESH)
    pl.semaphore_wait(barrier, PLANE + LINE - 2)

    def slot(buf, h, first, second, cols):
        owner = tgt_at(*at(h, first, second))
        return buf.at[pl.ds(pl.multiple_of(owner * 16 + 8 * h, 8), 8), cols]

    class Gather:
        shifts = (0, -1, 1, 2)

        def __init__(self, own, buf, c0, width):
            self.buf, self.c0, self.width = buf, c0, width
            self.full = pl.ds(c0, width)
            self.parts = (pl.ds(c0, width // 2), pl.ds(c0 + width // 2, width // 2))
            self.c = {}
            for h in (0, 1):
                mine = own.at[pl.ds(8 * h, 8), self.full]
                dst = slot(buf, h, 0, 0, self.full)
                for d in (1, -1):
                    self.c[h, "p1", d] = send(mine, dst, plane_dev(*at(h, d, 0)))
                    self.c[h, 0, d] = send(mine, dst, plane_dev(*at(h, 0, d)))

        def spread(self, h, j):
            ref = slot(self.buf, h, self.shifts[j], 0, self.full)
            for d in (1, -1):
                self.c[h, j, d] = send(ref, ref, plane_dev(*at(h, 0, d)))

        def first_ring(self):
            for d in (1, -1):
                for h in (0, 1):
                    self.c[h, "p1", d].wait_recv()
                    ref = slot(self.buf, h, -d, 0, self.parts[0 if d == 1 else 1])
                    self.c[h, "f1", d] = send(ref, ref, plane_dev(*at(h, d, 0)))
                    self.spread(h, 1 if d == 1 else 2)

        def forward(self, h, j):
            for d in (1, -1):
                self.c[h, j, d].wait_recv()
                ref = slot(self.buf, h, self.shifts[j], -d, self.parts[0 if d == 1 else 1])
                self.c[h, j, "f", d] = send(ref, ref, plane_dev(*at(h, 0, d)))

        def second_ring(self):
            for h in (0, 1):
                self.forward(h, 0)
            for h in (0, 1):
                self.c[h, "f1", 1].wait_recv()
                self.c[h, "f1", -1].wait_recv()
                self.spread(h, 3)
            for j in (1, 2, 3):
                for h in (0, 1):
                    self.forward(h, j)

        def finish(self):
            for j in range(4):
                for h in (0, 1):
                    for d in (1, -1):
                        self.c[h, j, "f", d].wait_recv()

    def to_plane(buf, row):
        buf[me_t] = row
        out = []
        for k in range(1, PLANE):
            ref = buf.at[me_t]
            out.append(send(ref, ref, (me_s, lax.rem(me_t + k, PLANE))))
        return out

    def to_line(buf, row):
        buf[me_s] = row
        out = []
        for k in range(1, LINE):
            ref = buf.at[me_s]
            out.append(send(ref, ref, (lax.rem(me_s + k, LINE), me_t)))
        return out

    def arrived(copies):
        for copy in copies:
            copy.wait_recv()

    def lse_over_first(a):
        top = jnp.max(a, axis=0)
        return top + jnp.log(jnp.sum(jnp.exp2(a - top[None]), axis=0)) * LOG2E

    def as_column(row, ref):
        for b in range(COLS // 128):
            piece = row[:, 128 * b : 128 * b + 128]
            ref[128 * b : 128 * b + 128, :] = jnp.broadcast_to(piece, (128, 128)).T

    def column_top(ref):
        return jnp.concatenate([ref[128 * b : 128 * b + 128, :].T[0:1, :] for b in range(COLS // 128)], axis=1)

    def column_sum(ref):
        return jnp.concatenate(
            [jnp.sum(ref[128 * b : 128 * b + 128, :].T, axis=0, keepdims=True) for b in range(COLS // 128)], axis=1
        )

    def tslot(dy, other, cols):
        k = wrap(y + dy) * 2 + (1 - core if other else core)
        return tg.at[pl.ds(pl.multiple_of(k * 32, 32), 32), cols]

    def line_dev(dy, other):
        return (wrap(y + dy) * 2 + (1 - core if other else core), me_t)

    all_cols = pl.ds(0, COLS)
    thalf = (pl.ds(0, COLS // 2), pl.ds(COLS // 2, COLS // 2))
    tcopy = {}
    for d in (1, -1):
        tcopy["y", d] = send(tgt, tslot(0, False, all_cols), line_dev(d, False))
    sgather = Gather(src, sg, 0, ROWS)
    tcopy["c", 0] = send(tgt, tslot(0, False, all_cols), line_dev(0, True))
    tg[pl.ds(pl.multiple_of(me_s * 32, 32), 32), :] = tgt[...]
    sg[pl.ds(pl.multiple_of(me_t * 16, 16), 16), :] = src[...]
    for d in (1, -1):
        tcopy["y", d].wait_recv()
        ref = tslot(-d, False, thalf[0 if d == 1 else 1])
        tcopy["f", d] = send(ref, ref, line_dev(d, False))
        ref = tslot(-d, False, all_cols)
        tcopy["c", -d] = send(ref, ref, line_dev(0, True))
    sgather.first_ring()
    tcopy["f", 1].wait_recv()
    tcopy["f", -1].wait_recv()
    ref = tslot(2, False, all_cols)
    tcopy["c", 2] = send(ref, ref, line_dev(0, True))
    sgather.second_ring()
    for d in (0, 1, -1, 2):
        tcopy["c", d].wait_recv()

    half_t = 0.5 * jnp.sum(tg[...] * tg[...], axis=0, keepdims=True)
    for b in range(COLS // 128):
        here = slice(128 * b, 128 * b + 128)
        high, low = halves(tg[:, here].T * SCALE)
        tcat[here, 0:256] = high
        tcat[here, 256:512] = high
        tcat[here, 512:768] = low
    as_column(half_t * SCALE, cb)

    sgather.finish()

    def split_points(buf, n, width):
        cols = pl.ds(pl.multiple_of(n * width, width), width)
        a = buf[:, cols]
        high, low = halves(a)
        scat[0:256, cols] = high
        scat[256:512, cols] = low
        scat[512:768, cols] = high
        return 0.5 * jnp.sum(a * a, axis=0, keepdims=True)

    WIDTH = 256

    def cross_step(n, _):
        cols = pl.ds(pl.multiple_of(n * WIDTH, WIDTH), WIDTH)
        frow[:, cols] = split_points(sg, n, WIDTH)
        cross = jnp.dot(tcat[...], scat[:, cols], preferred_element_type=F32)
        bias = cb[...]
        scores = cross - jnp.concatenate([bias, bias], axis=1)
        q[:, cols] = scores
        phi[:, cols] = jnp.max(scores, axis=0, keepdims=True)
        return 0

    lax.fori_loop(0, ROWS // WIDTH, cross_step, 0)

    def row_pass(body):
        def step(r, acc):
            return acc + body(pl.ds(pl.multiple_of(r * 8, 8), 8))

        acc = lax.fori_loop(0, COLS // 8, step, jnp.zeros((8, ROWS), F32), unroll=4)
        return jnp.sum(acc, axis=0, keepdims=True)

    top = phi[...]
    total = row_pass(lambda rows: jnp.exp2(q[rows, :] - top))
    copies = to_plane(vr.at[0], top + jnp.log(total) * LOG2E)
    arrived(copies)
    lse = lse_over_first(vr[0])
    phi[...] = slw[...] * LOG2E - lse
    frow[...] = frow[...] + EPSILON * (slw[...] - LN2 * lse)

    def col_pass(keep):
        def step(r, _):
            rows = pl.ds(pl.multiple_of(r * 8, 8), 8)
            scores = q[rows, :] + phi[...]
            top = jnp.max(scores, axis=1, keepdims=True)
            p = jnp.exp2(scores - top)
            if keep:
                e[rows, :] = p
            nb[rows, :] = jnp.broadcast_to(top, (8, 128))
            sb[rows, :] = functools.reduce(lambda a, b: a + b, [p[:, 128 * k : 128 * k + 128] for k in range(16)])
            return 0

        lax.fori_loop(0, COLS // 8, step, 0, unroll=4)
        return column_top(nb), column_sum(sb)

    ntop, total = col_pass(True)
    copies = to_line(vc.at[0], ntop + jnp.log(total) * LOG2E)
    arrived(copies)
    factor = jnp.exp2(ntop + (tlw[...] * LOG2E - lse_over_first(vc[0])))
    as_column(factor, cb)

    def against_column(rows):
        c = cb[rows, :]
        return e[rows, :] * jnp.concatenate([c] * 16, axis=1)

    copies = to_plane(vr.at[1], row_pass(against_column))
    arrived(copies)
    total = jnp.sum(vr[1], axis=0)
    f2 = frow[...] + EPSILON * (slw[...] - jnp.log(total))
    rowp[...] = f2
    phi[...] = jnp.exp(slw[...]) / total

    def weigh_step(r, _):
        rows = pl.ds(pl.multiple_of(r * 8, 8), 8)
        p = e[rows, :] * phi[...]
        sb[rows, :] = functools.reduce(lambda a, b: a + b, [p[:, 128 * k : 128 * k + 128] for k in range(16)])
        return 0

    lax.fori_loop(0, COLS // 8, weigh_step, 0, unroll=4)
    copies = to_line(vc.at[1], factor * column_sum(sb))
    arrived(copies)
    dual = factor * (jnp.exp(tlw[...]) / jnp.sum(vc[1], axis=0))
    as_column(dual, cb)

    copies = to_plane(vr.at[2], row_pass(against_column))
    high, low = halves(tg[...] * dual)
    tw[0:256, :] = high
    tw[256:512, :] = low
    BLOCK = 512
    for n in range(ROWS // BLOCK):
        cols = slice(n * BLOCK, n * BLOCK + BLOCK)

        def split_step(r, _):
            rows = pl.ds(pl.multiple_of(r * 16, 16), 16)
            high, low = halves(e[rows, cols])
            eh[rows, :] = high
            el[rows, :] = low
            return 0

        lax.fori_loop(0, COLS // 16, split_step, 0, unroll=4)
        acc = jnp.dot(tw[0:256, :], eh[...], preferred_element_type=F32)
        acc = acc + jnp.dot(tw[0:256, :], el[...], preferred_element_type=F32)
        acc = acc + jnp.dot(tw[256:512, :], eh[...], preferred_element_type=F32)
        w[:, :, :, :, cols] = acc.reshape(SIDE, SIDE, 2, 8, BLOCK)

    first_half, second_half = pl.ds(0, ROWS // 2), pl.ds(ROWS // 2, ROWS // 2)

    def group(h, shift):
        return (slice(None), wrap(z + shift), 0) if h == 0 else (wrap(x + shift), slice(None), 1)

    def single(h, shift):
        return (wrap(x + shift), z, 0) if h == 0 else (x, wrap(z + shift), 1)

    def cut(index, cols):
        return (*index, slice(None), cols)

    c = {}
    for h in (0, 1):
        for d, part in ((1, first_half), (-1, second_half)):
            c[h, "a", d] = send(w.at[cut(group(h, 2), part)], r1.at[h, :, :, part], plane_dev(*at(h, 0, d)))
    for h in (0, 1):
        for d, part in ((1, first_half), (-1, second_half)):
            c[h, "a", d].wait_recv()
            ref = w.at[cut(group(h, d), part)]
            ref[...] = ref[...] + r1[h, :, :, part]
            c[h, "b", d] = send(w.at[cut(group(h, d), pl.ds(0, ROWS))], r2.at[h, 0 if d == 1 else 1], plane_dev(*at(h, 0, d)))
    for h in (0, 1):
        c[h, "b", 1].wait_recv()
        c[h, "b", -1].wait_recv()
        ref = w.at[group(h, 0)]
        ref[...] = ref[...] + r2[h, 0] + r2[h, 1]
        for d, part in ((1, first_half), (-1, second_half)):
            c[h, "c", d] = send(w.at[cut(single(h, 2), part)], q1.at[h, :, part], plane_dev(*at(h, d, 0)))
    for h in (0, 1):
        for d, part in ((1, first_half), (-1, second_half)):
            c[h, "c", d].wait_recv()
            ref = w.at[cut(single(h, d), part)]
            ref[...] = ref[...] + q1[h, :, part]
            c[h, "d", d] = send(w.at[cut(single(h, d), pl.ds(0, ROWS))], q2.at[h, 0 if d == 1 else 1], plane_dev(*at(h, d, 0)))
    arrived(copies)
    ratio = tim[...] / jnp.sum(vr[2], axis=0)
    for h in (0, 1):
        c[h, "d", 1].wait_recv()
        c[h, "d", -1].wait_recv()
        share = w[single(h, 0)] + q2[h, 0] + q2[h, 1]
        moved[8 * h : 8 * h + 8, :] = (1.0 - tim[...]) * src[8 * h : 8 * h + 8, :] + ratio * share

    mgather = Gather(moved, mg, 0, ROWS)
    mg[pl.ds(pl.multiple_of(me_t * 16, 16), 16), :] = moved[...]
    mgather.first_ring()
    mgather.second_ring()
    mgather.finish()

    def last_step(n, _):
        cols = pl.ds(pl.multiple_of(n * WIDTH, WIDTH), WIDTH)
        phi[:, cols] = (rowp[:, cols] - split_points(mg, n, WIDTH)) * SCALE
        q[:, cols] = jnp.dot(tcat[...], scat[:, cols], preferred_element_type=F32)
        return 0

    lax.fori_loop(0, ROWS // WIDTH, last_step, 0)
    ntop, total = col_pass(False)
    copies = to_line(vc.at[2], ntop + jnp.log(total) * LOG2E)
    arrived(copies)
    colp[...] = EPSILON * (tlw[...] - LN2 * lse_over_first(vc[2])) + half_t

    for copy in started:
        copy.wait_send()


def per_device(sources, targets, source_logw, target_logw, times):
    vmem = pl.BlockSpec(memory_space=pltpu.VMEM)
    rowp, moved, colp = pl.pallas_call(
        kernel,
        out_shape=(
            jax.ShapeDtypeStruct((1, ROWS), F32),
            jax.ShapeDtypeStruct((16, ROWS), F32),
            jax.ShapeDtypeStruct((1, COLS), F32),
        ),
        in_specs=[vmem] * 5,
        out_specs=(vmem,) * 3,
        scratch_shapes=[
            pltpu.VMEM((FEATURES, ROWS), F32),
            pltpu.VMEM((FEATURES, COLS), F32),
            pltpu.VMEM((FEATURES, ROWS), F32),
            pltpu.VMEM((COLS, 3 * FEATURES), BF16),
            pltpu.VMEM((3 * FEATURES, ROWS), BF16),
            pltpu.VMEM((COLS, ROWS), F32),
            pltpu.VMEM((COLS, ROWS), F32),
            pltpu.VMEM((SIDE, SIDE, 2, 8, ROWS), F32),
            pltpu.VMEM((2 * FEATURES, COLS), BF16),
            pltpu.VMEM((COLS, 512), BF16),
            pltpu.VMEM((COLS, 512), BF16),
            pltpu.VMEM((2, SIDE, 8, ROWS), F32),
            pltpu.VMEM((2, 2, SIDE, 8, ROWS), F32),
            pltpu.VMEM((2, 8, ROWS), F32),
            pltpu.VMEM((2, 2, 8, ROWS), F32),
            pltpu.VMEM((3, PLANE, 1, ROWS), F32),
            pltpu.VMEM((3, LINE, 1, COLS), F32),
            pltpu.VMEM((COLS, 128), F32),
            pltpu.VMEM((COLS, 128), F32),
            pltpu.VMEM((COLS, 128), F32),
            pltpu.VMEM((1, ROWS), F32),
            pltpu.VMEM((1, ROWS), F32),
            pltpu.VMEM((1, ROWS), F32),
            pltpu.SemaphoreType.DMA((COPIES,)),
            pltpu.SemaphoreType.DMA((COPIES,)),
        ],
        compiler_params=pltpu.CompilerParams(
            collective_id=0, has_side_effects=True, vmem_limit_bytes=60 * 1024 * 1024
        ),
    )(sources, targets, source_logw[None], target_logw[None], times[None])
    return rowp[0], moved, colp[0]


def solution(mesh):
    return jax.shard_map(
        per_device,
        mesh=mesh,
        in_specs=(P("tgt", "src"), P("src", "tgt"), P("src"), P("tgt"), P("src")),
        out_specs=(P("src"), P("tgt", "src"), P("tgt")),
        check_vma=False,
    )
```

time: 322 us -> 125 us (0.39)
  Pallas kernels: 0 us -> 121 us
  matrix products: 83.3 us -> 0 us
  waiting for transfers between devices: 69.6 us -> 0 us
  blocking collectives: 64.5 us -> 0 us
  starting transfers between devices: 36.2 us -> 0 us
  other arithmetic: 31.7 us -> 0 us
  local copies, waits for them, and re-layouts: 18.7 us -> 3.45 us
  between operations: 14.7 us -> 0.65 us
    pallas_call x0 -> x1, Pallas kernels: none -> 121 us  [per_device(): pl.pallas_call(kernel, out_shape=(jax.ShapeDtypeStruct((1, ROWS), F32), j...]
    dot_general x28 -> x0, matrix products: 83.3 us -> none  [the longest x24 72.8 us: cost_block(): jnp.dot(rows, cols.T, precision=lax.Precision.HIGHEST, preferred_element_...]
    all_to_all x7 -> x0, waiting for transfers between devices: 60.9 us -> none  [the longest x6 60.9 us: from_everyone(): return lax.all_to_all(copies, axis, split_axis=0, concat_axis=0, tiled=True)]
    all_to_all x7 -> x0, starting transfers between devices: 36.2 us -> none  [the longest x6 32.3 us: from_everyone(): return lax.all_to_all(copies, axis, split_axis=0, concat_axis=0, tiled=True)]
    psum x2 -> x0, blocking collectives: 36 us -> none  [by_axis(): shard = lax.psum(shard, axis)]
    reduce_sum x46 -> x0, other arithmetic: 28.7 us -> none  [the longest x12 16.6 us: step(): jnp.sum(jnp.exp(scores - fresh[None, :]), 0)]
    all_gather x1 -> x0, blocking collectives: 14.3 us -> none  [gather_axes(): nearer = lax.all_gather(shard, axes[-1], axis=dim, tiled=True)]
    all_to_all x1 -> x0, blocking collectives: 14.2 us -> none  [from_everyone(): return lax.all_to_all(copies, axis, split_axis=0, concat_axis=0, tiled=True)]
  transfers between devices with their start and end apart: 8 -> 0, of which waited for: 7 -> 0; matrix products, arithmetic and copies ran while one was open for 1% -> 0% of each run, Pallas kernels for 0% -> 0%
where the time goes in v1:
time: 125 us
  Pallas kernels  121 us (97%)
  local copies, waits for them, and re-layouts  3.45 us (3%)
    pallas_call x1, Pallas kernels, per_device(): pl.pallas_call(kernel, out_shape=(jax.ShapeDtypeStruct((1, ROWS), F32), j...  121 us
    unnamed x7, local copies, waits for them, and re-layouts  3.45 us

profile of v1, /device:TPU:1, one launch (start us, length us, event | category | flops | bytes accessed | tf_op | source)
XLA Modules:
  0.0 125.1 jit_solution(12476369793817115836)
XLA Ops:
  0.6 121.0 %shard_map.76 = (f32[1,2048]{1,0:T(1,128)}, f32[16,2048]{1,0:T(8,128)}, f32[1,1024]{1,0:T(1,128)}) custom-call(f32[16,2048]{1,0:T(8,128)} %src.1, f32[32,1024]{1,0:T(8,128)} %tgt.1, f32[1,2048]{1,0:T(1,128)} %bitcast.5, f32[1,1024]{1,0:T(1,128)} %bitcast.8, f32[1,2048]{1,0:T(1,128)} %bitcast.6), custom_call_target="tpu_custom_call" | custom-call | tf_op jit(solution)/shard_map/pallas_call | solution.py:376
  121.6 0.0 copy-start
  121.6 0.7 copy-done
  122.3 0.6 copy.11
  122.9 0.0 copy-start.1
  122.9 1.6 %copy.12 = f32[16,2048]{1,0:T(8,128)} copy(f32[16,2048]{1,0:T(8,128)} %get-tuple-element.13) | data formatting | bytes 262144
  124.5 0.0 copy-done.1
  124.5 0.6 copy.13
Async XLA Ops:
  121.6 0.7 copy-start
  122.9 1.6 %copy-start.1 = (f32[1,1024]{1,0:T(1,128)S(1)}, f32[1,1024]{1,0:T(1,128)}, u32[]{:S(2)}) copy-start(f32[1,1024]{1,0:T(1,128)} %get-tuple-element.8) | copy-start | bytes 12292

commit v2 on v1

v2 whole, which is shorter than its diff:
```python
import functools

import jax
import jax.numpy as jnp
from jax import lax
from jax.experimental import pallas as pl
from jax.experimental.pallas import tpu as pltpu
from jax.sharding import PartitionSpec as P

MESH = pl.DeviceIdType.MESH
F32 = jnp.float32
BF16 = jnp.bfloat16
EPSILON = 16.0
LOG2E = 1.4426950408889634
LN2 = 0.6931471805599453
SCALE = LOG2E / EPSILON

FEATURES = 256
ROWS = 2048
COLS = 1024
SIDE = 4
GROUP = 16
LINE = 8
COPIES = 256
CHUNKS = 2
CHUNK = ROWS // CHUNKS
WIDTH = 256


def halves(a):
    high = a.astype(BF16)
    return high, (a - high.astype(F32)).astype(BF16)


def tiles(a):
    return functools.reduce(lambda p, r: p + r, [a[:, 128 * k : 128 * k + 128] for k in range(ROWS // 128)])


def kernel(
    src_h, tgt_h, slw_h, tlw_h, tim_h,
    rowp, moved, colp,
    src, tgt, own, far, slw, tlw, tim, sg, tg, mg, mv, tcat, scat, q, e, w, tw, eh, el,
    r0, rb, rx1, rx2, qb, vr, vc, nb, sb, cb, part, frow, phi, f2, ff,
    send_sem, recv_sem, in_sem,
):
    me_s, me_t = lax.axis_index("src"), lax.axis_index("tgt")
    x, z = me_t // SIDE, me_t % SIDE
    y, core = me_s // 2, me_s % 2
    block = z // 2
    mate = z + 1 - 2 * (z % 2)
    opp = SIDE - 1 - z
    other = 1 - core
    mine = core == block
    started = []

    def wrap(value):
        return lax.rem(value + SIDE, SIDE)

    def dev(dx=0, dy=0, zz=z, cc=core):
        return (wrap(y + dy) * 2 + cc, wrap(x + dx) * SIDE + zz)

    def copy_to(source, target, device, k):
        return pltpu.make_async_remote_copy(
            src_ref=source, dst_ref=target, send_sem=send_sem.at[k], recv_sem=recv_sem.at[k],
            device_id=device, device_id_type=MESH,
        )

    count = [0]

    def number():
        count[0] += 1
        return count[0] - 1

    def send(source, target, device):
        copy = copy_to(source, target, device, number())
        copy.start()
        started.append(copy)
        return copy

    loads = [
        pltpu.make_async_copy(a, b, in_sem.at[k])
        for k, (a, b) in enumerate(((src_h, src), (tgt_h, tgt), (slw_h, own.at[0]), (tim_h, own.at[1]), (tlw_h, own.at[2, :, pl.ds(0, COLS)])))
    ]
    for load in loads:
        load.start()
    barrier = pltpu.get_barrier_semaphore()
    near = [dev(1), dev(-1), dev(dy=1), dev(dy=-1), dev(zz=mate), dev(zz=opp), dev(zz=opp, cc=other), dev(cc=other)]
    for device in near:
        pl.semaphore_signal(barrier, inc=1, device_id=device, device_id_type=MESH)
    for load in loads:
        load.wait()
    pl.semaphore_wait(barrier, len(near))

    def slot(buf, dx, zz, cc, cols):
        return buf.at[pl.ds(pl.multiple_of((wrap(x + dx) * SIDE + zz) * 16 + 8 * cc, 8), 8), cols]

    def chunk_cols(n):
        return pl.ds(n * CHUNK, CHUNK)

    def chunk_half(n, d):
        return pl.ds(n * CHUNK + (0 if d == 1 else CHUNK // 2), CHUNK // 2)

    class Gather:
        def __init__(self, buf, n):
            self.buf, self.n = buf, n
            self.cols = chunk_cols(n)
            self.c = {}
            self.local = []

        def share(self, dx, zz):
            ref = slot(self.buf, dx, zz, core, self.cols)
            self.local.append(send(ref, ref, dev(cc=other)))

        def to_mate(self, key, dx, zz):
            ref = slot(self.buf, dx, zz, core, self.cols)
            self.c[key] = send(ref, ref, dev(zz=mate))

        def round_x(self, key, zz):
            ref = slot(self.buf, 0, zz, core, self.cols)
            for d in (1, -1):
                self.c[key, d] = send(ref, ref, dev(d))

        def onward(self, key, zz):
            for d in (1, -1):
                self.c[key, d].wait_recv()
                ref = slot(self.buf, -d, zz, core, chunk_half(self.n, d))
                self.c[key, "f", d] = send(ref, ref, dev(d))

        def end_of_round(self, key):
            for d in (1, -1):
                self.c[key, "f", d].wait_recv()

        def start_near(self):
            self.round_x("n", z)
            self.to_mate(("m", 0), 0, z)
            self.share(0, z)

        def start_far(self):
            self.to_mate("fm", 0, opp)
            self.round_x("f", opp)
            self.share(0, opp)

        def step1(self):
            self.onward("n", z)
            for d in (1, -1):
                self.to_mate(("m", -d), -d, z)
                self.share(-d, z)

        def step2(self):
            self.c["fm"].wait_recv()
            self.round_x("g", SIDE - 1 - mate)
            self.share(0, SIDE - 1 - mate)
            self.onward("f", opp)
            for d in (1, -1):
                self.share(-d, opp)

        def step3(self):
            self.end_of_round("n")
            self.to_mate(("m", 2), 2, z)
            self.share(2, z)
            self.c["m", 0].wait_recv()
            self.share(0, mate)
            self.onward("g", SIDE - 1 - mate)
            for d in (1, -1):
                self.share(-d, SIDE - 1 - mate)

        def step4(self):
            self.end_of_round("f")
            self.share(2, opp)
            for d in (1, -1, 2):
                self.c["m", d].wait_recv()
                self.share(d, mate)
            self.end_of_round("g")
            self.share(2, SIDE - 1 - mate)

        def finish(self):
            for copy in self.local:
                copy.wait_recv()

    def group_devices():
        return [
            dev(dx, zz=zz, cc=cc)
            for dx in (2, 1, -1, 0)
            for zz in (mate, z)
            for cc in (other, core)
            if not (dx == 0 and zz is z and cc is core)
        ]

    group_slot = x * 4 + (z % 2) * 2 + core
    line_slot = y * 2 + block

    def to_all(buf, k, row, devices):
        buf[k] = row
        return [send(buf.at[k], buf.at[k], device) for device in devices]

    def to_group(buf, row):
        return to_all(buf, group_slot, row, group_devices())

    line = [(dy, zz, cc) for dy in (2, 1, -1, 0) for zz, cc in ((opp, other), (z, core)) if not (dy == 0 and zz is z)]

    def to_line(buf, row):
        return to_all(buf, line_slot, row, [dev(dy=dy, zz=zz, cc=cc) for dy, zz, cc in line])

    def arrived(copies):
        for copy in copies:
            copy.wait_recv()

    def lse_over_first(a):
        top = jnp.max(a, axis=0)
        return top + jnp.log(jnp.sum(jnp.exp2(a - top[None]), axis=0)) * LOG2E

    def as_column(row, ref):
        for b in range(COLS // 128):
            piece = row[:, 128 * b : 128 * b + 128]
            ref[128 * b : 128 * b + 128, :] = jnp.broadcast_to(piece, (128, 128)).T

    def column_top(ref):
        return jnp.concatenate([ref[128 * b : 128 * b + 128, :].T[0:1, :] for b in range(COLS // 128)], axis=1)

    def column_sum(ref):
        return jnp.concatenate(
            [jnp.sum(ref[128 * b : 128 * b + 128, :].T, axis=0, keepdims=True) for b in range(COLS // 128)], axis=1
        )

    both = pl.ds(0, ROWS)
    k_near = number()
    k_far = (number(), number())

    def out_half(cc):
        return src.at[pl.ds(pl.multiple_of(8 * cc, 8), 8), :]

    give_near = copy_to(out_half(other), slot(sg, 0, z, other, both), dev(cc=other), k_near)
    give_far = [copy_to(out_half(0), slot(sg, 0, z, 0, both), dev(zz=opp, cc=0), k_far[0]), None]
    take_near = copy_to(out_half(0), slot(sg, 0, z, core, both), dev(cc=other), k_near)
    take_far = copy_to(out_half(0), slot(sg, 0, opp, core, both), dev(zz=opp), k_far[0])
    give_far[1] = pltpu.make_async_remote_copy(
        src_ref=out_half(1), dst_ref=slot(sg, 0, z, 1, both), send_sem=send_sem.at[k_far[1]], recv_sem=recv_sem.at[k_far[0]],
        device_id=dev(zz=opp, cc=1), device_id_type=MESH,
    )

    k_t = (number(), number())

    def tslot(dy, cc, rows=None):
        start, size = (0, 32) if rows is None else rows
        return tg.at[pl.ds(pl.multiple_of(64 * wrap(y + dy) + 32 * cc + start, 16), size), :]

    def tcopy(device, k):
        return pltpu.make_async_remote_copy(
            src_ref=tgt, dst_ref=tslot(0, core), send_sem=send_sem.at[k], recv_sem=recv_sem.at[k_t[0] + core],
            device_id=device, device_id_type=MESH,
        )

    give_t = tcopy(dev(zz=opp, cc=1), k_t[0])
    give_t_here = tcopy(dev(cc=0), k_t[1])
    take_t = [copy_to(tgt, tslot(0, cc), dev(zz=opp, cc=1), k_t[cc]) for cc in (0, 1)]

    give_t.start()

    @pl.when(core == 1)
    def _():
        give_t_here.start()

    @pl.when(mine)
    def _():
        give_near.start()

    @pl.when(jnp.logical_not(mine))
    def _():
        give_far[0].start()
        give_far[1].start()

    small = [
        send(own.at[0], far.at[0], dev(cc=other)),
        send(own.at[1], far.at[1], dev(cc=other)),
        send(own.at[2, :, pl.ds(0, COLS)], far.at[2, :, pl.ds(0, COLS)], dev(zz=opp)),
    ]

    @pl.when(mine)
    def _():
        slot(sg, 0, z, core, both)[...] = out_half(core)[...]

    @pl.when(core == 0)
    def _():
        tslot(0, 0)[...] = tgt[...]

    @pl.when(jnp.logical_not(mine))
    def _():
        take_near.wait_recv()

    gathers = [Gather(sg, n) for n in range(CHUNKS)]
    for g in gathers:
        g.start_near()

    @pl.when(core == 1)
    def _():
        take_t[0].wait_recv()

    yc = {}
    for cc in (0, 1):
        if cc == 1:
            take_t[1].wait_recv()
        for d in (1, -1):
            yc[cc, d] = send(tslot(0, cc), tslot(0, cc), dev(dy=d))
    take_far.wait_recv()
    for g in gathers:
        g.start_far()
    gathers[0].step1()
    for cc in (0, 1):
        for d in (1, -1):
            yc[cc, d].wait_recv()
            ref = tslot(-d, cc, (0 if d == 1 else 16, 16))
            yc[cc, "f", d] = send(ref, ref, dev(dy=d))
    for g in gathers[1:]:
        g.step1()
    for g in gathers:
        g.step2()
    for g in gathers[:-1]:
        g.step3()
    for cc in (0, 1):
        for d in (1, -1):
            yc[cc, "f", d].wait_recv()

    half_t = 0.5 * jnp.sum(tg[...] * tg[...], axis=0, keepdims=True)
    for b in range(COLS // 128):
        here = slice(128 * b, 128 * b + 128)
        high, low = halves(tg[:, here].T * SCALE)
        tcat[here, 0:256] = high
        tcat[here, 256:512] = high
        tcat[here, 512:768] = low
    as_column(half_t * SCALE, cb)

    gathers[-1].step3()
    for g in gathers[:-1]:
        g.step4()

    def split_points(buf, n):
        cols = pl.ds(pl.multiple_of(n * WIDTH, WIDTH), WIDTH)
        a = buf[:, cols]
        high, low = halves(a)
        scat[0:256, cols] = high
        scat[256:512, cols] = low
        scat[512:768, cols] = high
        return 0.5 * jnp.sum(a * a, axis=0, keepdims=True)

    def cross_step(n, _):
        cols = pl.ds(pl.multiple_of(n * WIDTH, WIDTH), WIDTH)
        frow[:, cols] = split_points(sg, n)
        cross = jnp.dot(tcat[...], scat[:, cols], preferred_element_type=F32)
        bias = cb[...]
        scores = cross - jnp.concatenate([bias, bias], axis=1)
        q[:, cols] = scores
        phi[:, cols] = jnp.max(scores, axis=0, keepdims=True)
        return 0

    def over_chunk(n, step):
        lax.fori_loop(n * CHUNK // WIDTH, (n + 1) * CHUNK // WIDTH, step, 0)

    for n, g in enumerate(gathers):
        if n == CHUNKS - 1:
            g.step4()
        g.finish()
        over_chunk(n, cross_step)

    arrived(small)
    slw[...] = jnp.where(mine, own[0], far[0])
    tim[...] = jnp.where(mine, own[1], far[1])
    tlw[...] = jnp.where(core == 0, own[2], far[2])[:, 0:COLS]

    give_t.wait_send()

    @pl.when(core == 1)
    def _():
        give_t_here.wait_send()

    @pl.when(mine)
    def _():
        give_near.wait_send()

    @pl.when(jnp.logical_not(mine))
    def _():
        give_far[0].wait_send()
        give_far[1].wait_send()

    def row_pass(body):
        def step(r, acc):
            return acc + body(pl.ds(pl.multiple_of(r * 8, 8), 8))

        acc = lax.fori_loop(0, COLS // 8, step, jnp.zeros((8, ROWS), F32), unroll=4)
        return jnp.sum(acc, axis=0, keepdims=True)

    top = phi[...]
    total = row_pass(lambda rows: jnp.exp2(q[rows, :] - top))
    copies = to_group(vr.at[0], top + jnp.log(total) * LOG2E)
    arrived(copies)
    lse = lse_over_first(vr[0])
    phi[...] = slw[...] * LOG2E - lse
    frow[...] = frow[...] + EPSILON * (slw[...] - LN2 * lse)

    def col_pass(keep):
        def top_step(r, _):
            rows = pl.ds(pl.multiple_of(r * 8, 8), 8)
            scores = q[rows, :] + phi[...]
            nb[rows, :] = functools.reduce(jnp.maximum, [scores[:, 128 * k : 128 * k + 128] for k in range(ROWS // 128)])
            return 0

        lax.fori_loop(0, COLS // 8, top_step, 0, unroll=4)

        def join_step(r, _):
            rows = pl.ds(pl.multiple_of(r * 128, 128), 128)
            nb[rows, :] = jnp.broadcast_to(jnp.max(nb[rows, :], axis=1, keepdims=True), (128, 128))
            return 0

        lax.fori_loop(0, COLS // 128, join_step, 0)

        def step(r, _):
            rows = pl.ds(pl.multiple_of(r * 8, 8), 8)
            p = jnp.exp2(q[rows, :] + phi[...] - jnp.concatenate([nb[rows, :]] * (ROWS // 128), axis=1))
            if keep:
                e[rows, :] = p
            sb[rows, :] = tiles(p)
            return 0

        lax.fori_loop(0, COLS // 8, step, 0, unroll=4)
        return column_top(nb), column_sum(sb)

    ntop, total = col_pass(True)
    copies = to_line(vc.at[0], ntop + jnp.log(total) * LOG2E)
    arrived(copies)
    factor = jnp.exp2(ntop + (tlw[...] * LOG2E - lse_over_first(vc[0])))
    as_column(factor, cb)

    def against_column(rows):
        return e[rows, :] * jnp.concatenate([cb[rows, :]] * (ROWS // 128), axis=1)

    copies = to_group(vr.at[1], row_pass(against_column))
    arrived(copies)
    total = jnp.sum(vr[1], axis=0)
    f2[...] = frow[...] + EPSILON * (slw[...] - jnp.log(total))
    phi[...] = jnp.exp(slw[...]) / total
    potential = send(f2, ff, dev(zz=opp))

    def weigh_step(r, _):
        rows = pl.ds(pl.multiple_of(r * 8, 8), 8)
        sb[rows, :] = tiles(e[rows, :] * phi[...])
        return 0

    lax.fori_loop(0, COLS // 8, weigh_step, 0, unroll=4)
    copies = to_line(vc.at[1], factor * column_sum(sb))
    arrived(copies)
    dual = factor * (jnp.exp(tlw[...]) / jnp.sum(vc[1], axis=0))
    as_column(dual, cb)

    potential.wait_recv()

    copies = to_group(vr.at[2], row_pass(against_column))
    high, low = halves(tg[...] * dual)
    tw[0:256, :] = high
    tw[256:512, :] = low
    BLOCK = 512

    def wz(zz, cols, dx=None):
        return w.at[slice(None) if dx is None else wrap(x + dx), zz, core, :, cols]

    mates_opp = SIDE - 1 - mate
    c = {}
    for n in range(CHUNKS):
        for m in range(n * CHUNK // BLOCK, (n + 1) * CHUNK // BLOCK):
            cols = slice(m * BLOCK, m * BLOCK + BLOCK)

            def split_step(r, _):
                rows = pl.ds(pl.multiple_of(r * 16, 16), 16)
                high, low = halves(e[rows, cols])
                eh[rows, :] = high
                el[rows, :] = low
                return 0

            lax.fori_loop(0, COLS // 16, split_step, 0, unroll=4)
            acc = jnp.dot(tw[0:256, :], eh[...], preferred_element_type=F32)
            acc = acc + jnp.dot(tw[0:256, :], el[...], preferred_element_type=F32)
            acc = acc + jnp.dot(tw[256:512, :], eh[...], preferred_element_type=F32)
            w[:, :, :, :, cols] = acc.reshape(SIDE, SIDE, 2, 8, BLOCK)
        cols = chunk_cols(n)
        c[n, "core"] = send(w.at[:, :, other, :, cols], r0.at[:, :, :, cols], dev(cc=other))

    def rx_start(n, key, zz, k):
        for d in (1, -1):
            cut = chunk_half(n, d)
            c[n, key, d] = send(wz(zz, cut, 2), rx1.at[k, :, cut], dev(d))

    def rx_middle(n, key, zz, k):
        for d in (1, -1):
            cut = chunk_half(n, d)
            c[n, key, d].wait_recv()
            ref = wz(zz, cut, d)
            ref[...] = ref[...] + rx1[k, :, cut]
            c[n, key, "s", d] = send(wz(zz, chunk_cols(n), d), rx2.at[k, 0 if d == 1 else 1, :, chunk_cols(n)], dev(d))

    def rx_end(n, key, zz, k):
        for d in (1, -1):
            c[n, key, "s", d].wait_recv()
        cols = chunk_cols(n)
        return wz(zz, cols, 0)[...] + rx2[k, 0, :, cols] + rx2[k, 1, :, cols]

    def rs1(n):
        cols = chunk_cols(n)
        c[n, "core"].wait_recv()
        ref = w.at[:, :, core, :, cols]
        ref[...] = ref[...] + r0[:, :, :, cols]
        c[n, "mate"] = send(wz(mate, cols), rb.at[:, :, cols], dev(zz=mate))
        rx_start(n, "m", mates_opp, 0)
        rx_start(n, "o", opp, 1)

    def rs2(n):
        cols = chunk_cols(n)
        rx_middle(n, "m", mates_opp, 0)
        c[n, "mate"].wait_recv()
        ref = wz(z, cols)
        ref[...] = ref[...] + rb[:, :, cols]
        rx_start(n, "z", z, 2)
        rx_middle(n, "o", opp, 1)

    def rs3(n):
        cols = chunk_cols(n)
        qs = wz(mates_opp, cols, 0)
        qs[...] = rx_end(n, "m", mates_opp, 0)
        c[n, "last"] = send(qs, qb.at[:, cols], dev(zz=mate))
        rx_middle(n, "z", z, 2)

    def point_rows(zz):
        return pl.ds(pl.multiple_of((x * SIDE + zz) * 16 + 8 * core, 8), 8)

    mgathers = [Gather(mg, n) for n in range(CHUNKS)]
    k_out = [(number(), number()) for _ in range(CHUNKS)]
    outs = []

    def rs4(n):
        cols = chunk_cols(n)
        g = mgathers[n]
        ratio = tim[:, cols] / jnp.sum(vr[2, :, :, cols], axis=0)
        keep = 1.0 - tim[:, cols]
        share = rx_end(n, "o", opp, 1)
        c[n, "last"].wait_recv()
        mg[point_rows(opp), cols] = keep * sg[point_rows(opp), cols] + ratio * (share + qb[:, cols])
        g.start_far()
        share = rx_end(n, "z", z, 2)
        mg[point_rows(z), cols] = keep * sg[point_rows(z), cols] + ratio * share
        g.start_near()
        here = mv.at[pl.ds(pl.multiple_of(8 * core, 8), 8), cols]
        there = mv.at[pl.ds(pl.multiple_of(8 * other, 8), 8), cols]

        def result(zz, device, k):
            return pltpu.make_async_remote_copy(
                src_ref=slot(mg, 0, zz, core, cols), dst_ref=here, send_sem=send_sem.at[k], recv_sem=recv_sem.at[k_out[n][0] + core],
                device_id=device, device_id_type=MESH,
            )

        far_out = result(opp, dev(zz=opp, cc=block), k_out[n][0])
        near_out = result(z, dev(cc=other), k_out[n][1])
        far_out.start()
        started.append(far_out)

        @pl.when(mine)
        def _():
            here[...] = mg[point_rows(z), cols]

        @pl.when(jnp.logical_not(mine))
        def _():
            near_out.start()

        def result_in(ref, k):
            return pltpu.make_async_remote_copy(
                src_ref=ref, dst_ref=ref, send_sem=send_sem.at[k_out[n][0]], recv_sem=recv_sem.at[k],
                device_id=dev(cc=other), device_id_type=MESH,
            )

        outs.append((near_out, result_in(here, k_out[n][0] + core), result_in(there, k_out[n][0] + other)))

    order = [rs1, rs2, rs3]
    for stage in order:
        for n in range(CHUNKS):
            stage(n)
    arrived(copies)
    for n in range(CHUNKS):
        rs4(n)

    def last_step(n, _):
        cols = pl.ds(pl.multiple_of(n * WIDTH, WIDTH), WIDTH)
        phi[:, cols] = (f2[:, cols] - split_points(mg, n)) * SCALE
        q[:, cols] = jnp.dot(tcat[...], scat[:, cols], preferred_element_type=F32)
        return 0

    for name in ("step1", "step2", "step3"):
        for g in mgathers:
            getattr(g, name)()
    for n, g in enumerate(mgathers):
        g.step4()
        g.finish()
        over_chunk(n, last_step)
    ntop, total = col_pass(False)
    home = z + core * (opp - z)
    part[...] = ntop + jnp.log(total) * LOG2E - half_t * SCALE

    def to_owner(dy, cc, k, base):
        return pltpu.make_async_remote_copy(
            src_ref=part, dst_ref=vc.at[2, line_slot], send_sem=send_sem.at[k], recv_sem=recv_sem.at[base + core],
            device_id=dev(dy=dy, zz=home, cc=cc), device_id_type=MESH,
        )

    def from_owner(k):
        return copy_to(part, vc.at[2, line_slot], dev(cc=other), k)

    waits = []
    for dy in (2, 1, -1):
        base, more = number(), number()
        for cc, k in ((0, base), (1, more)):
            copy = to_owner(dy, cc, k, base)
            copy.start()
            started.append(copy)
        waits += [from_owner(base), from_owner(more)]
    base, more = number(), number()
    to_one, to_zero = to_owner(0, 1, more, base), to_owner(0, 0, base, base)
    to_one.start()
    started.append(to_one)

    @pl.when(core == 1)
    def _():
        to_zero.start()
        from_owner(base).wait_recv()

    @pl.when(core == 0)
    def _():
        vc[2, line_slot] = part[...]

    from_owner(more).wait_recv()
    arrived(waits)
    colp[...] = EPSILON * (own[2][:, 0:COLS] - LN2 * lse_over_first(vc[2]))

    rowp[...] = jnp.where(mine, f2[...], ff[...])
    for near_out, half_here, half_there in outs:
        half_there.wait_recv()

        @pl.when(jnp.logical_not(mine))
        def _():
            half_here.wait_recv()
            near_out.wait_send()

    moved[...] = mv[...]

    @pl.when(core == 1)
    def _():
        to_zero.wait_send()

    for copy in started:
        copy.wait_send()


def per_device(sources, targets, source_logw, target_logw, times):
    vmem, anywhere = pl.BlockSpec(memory_space=pltpu.VMEM), pl.BlockSpec(memory_space=pl.ANY)
    rowp, moved, colp = pl.pallas_call(
        kernel,
        out_shape=(
            jax.ShapeDtypeStruct((1, ROWS), F32),
            jax.ShapeDtypeStruct((16, ROWS), F32),
            jax.ShapeDtypeStruct((1, COLS), F32),
        ),
        in_specs=[anywhere] * 5,
        out_specs=(vmem,) * 3,
        scratch_shapes=[
            pltpu.VMEM((16, ROWS), F32),
            pltpu.VMEM((32, COLS), F32),
            pltpu.VMEM((3, 1, ROWS), F32),
            pltpu.VMEM((3, 1, ROWS), F32),
            pltpu.VMEM((1, ROWS), F32),
            pltpu.VMEM((1, COLS), F32),
            pltpu.VMEM((1, ROWS), F32),
            pltpu.VMEM((FEATURES, ROWS), F32),
            pltpu.VMEM((FEATURES, COLS), F32),
            pltpu.VMEM((FEATURES, ROWS), F32),
            pltpu.VMEM((16, ROWS), F32),
            pltpu.VMEM((COLS, 3 * FEATURES), BF16),
            pltpu.VMEM((3 * FEATURES, ROWS), BF16),
            pltpu.VMEM((COLS, ROWS), F32),
            pltpu.VMEM((COLS, ROWS), F32),
            pltpu.VMEM((SIDE, SIDE, 2, 8, ROWS), F32),
            pltpu.VMEM((2 * FEATURES, COLS), BF16),
            pltpu.VMEM((COLS, 512), BF16),
            pltpu.VMEM((COLS, 512), BF16),
            pltpu.VMEM((SIDE, SIDE, 8, ROWS), F32),
            pltpu.VMEM((SIDE, 8, ROWS), F32),
            pltpu.VMEM((3, 8, ROWS), F32),
            pltpu.VMEM((3, 2, 8, ROWS), F32),
            pltpu.VMEM((8, ROWS), F32),
            pltpu.VMEM((3, GROUP, 1, ROWS), F32),
            pltpu.VMEM((3, LINE, 1, COLS), F32),
            pltpu.VMEM((COLS, 128), F32),
            pltpu.VMEM((COLS, 128), F32),
            pltpu.VMEM((COLS, 128), F32),
            pltpu.VMEM((1, COLS), F32),
            pltpu.VMEM((1, ROWS), F32),
            pltpu.VMEM((1, ROWS), F32),
            pltpu.VMEM((1, ROWS), F32),
            pltpu.VMEM((1, ROWS), F32),
            pltpu.SemaphoreType.DMA((COPIES,)),
            pltpu.SemaphoreType.DMA((COPIES,)),
            pltpu.SemaphoreType.DMA((5,)),
        ],
        compiler_params=pltpu.CompilerParams(
            collective_id=0, has_side_effects=True, vmem_limit_bytes=60 * 1024 * 1024
        ),
    )(sources, targets, source_logw[None], target_logw[None], times[None])
    return rowp[0], moved, colp[0]


def solution(mesh):
    return jax.shard_map(
        per_device,
        mesh=mesh,
        in_specs=(P("tgt", "src"), P("src", "tgt"), P("src"), P("tgt"), P("src")),
        out_specs=(P("src"), P("tgt", "src"), P("tgt")),
        check_vma=False,
    )
```

time: 125 us -> 110 us (0.88)
  Pallas kernels: 121 us -> 106 us
    pallas_call x1, Pallas kernels: 121 us -> 106 us  [per_device(): pl.pallas_call(kernel, out_shape=(jax.ShapeDtypeStruct((1, ROWS), F32), j...]
where the time goes in v2:
time: 110 us
  Pallas kernels  106 us (96%)
  local copies, waits for them, and re-layouts  3.45 us (3%)
    pallas_call x1, Pallas kernels, per_device(): pl.pallas_call(kernel, out_shape=(jax.ShapeDtypeStruct((1, ROWS), F32), j...  106 us
    unnamed x7, local copies, waits for them, and re-layouts  3.45 us

profile of v2, /device:TPU:1, one launch (start us, length us, event | category | flops | bytes accessed | tf_op | source)
XLA Modules:
  0.0 110.2 jit_solution(8116636316841716971)
XLA Ops:
  0.6 106.1 %shard_map.76 = (f32[1,2048]{1,0:T(1,128)}, f32[16,2048]{1,0:T(8,128)}, f32[1,1024]{1,0:T(1,128)}) custom-call(f32[16,2048]{1,0:T(8,128)} %src_h.1, f32[32,1024]{1,0:T(8,128)} %tgt_h.1, f32[1,2048]{1,0:T(1,128)} %bitcast.5, f32[1,1024]{1,0:T(1,128)} %bitcast.8, f32[1,2048]{1,0:T(1,128)} %bitcast.6), custom_call_target="tpu_custom_call" | custom-call | tf_op jit(solution)/shard_map/pallas_call | solution.py:659
  106.7 0.0 copy-start
  106.7 0.7 copy-done
  107.4 0.6 copy.11
  108.0 0.0 copy-start.1
  108.0 1.6 %copy.12 = f32[16,2048]{1,0:T(8,128)} copy(f32[16,2048]{1,0:T(8,128)} %get-tuple-element.13) | data formatting | bytes 262144
  109.6 0.0 copy-done.1
  109.6 0.6 copy.13
Async XLA Ops:
  106.7 0.7 copy-start
  108.0 1.6 %copy-start.1 = (f32[1,1024]{1,0:T(1,128)S(1)}, f32[1,1024]{1,0:T(1,128)}, u32[]{:S(2)}) copy-start(f32[1,1024]{1,0:T(1,128)} %get-tuple-element.8) | copy-start | bytes 12292

commit v3 on v2

--- a/solution.py
+++ b/solution.py
@@ -25,6 +25,9 @@
 CHUNKS = 2
 CHUNK = ROWS // CHUNKS
 WIDTH = 256
+PARTS = 2
+PART = COLS // PARTS
+BLOCK = 512
 
 
 def halves(a):
@@ -33,14 +36,14 @@
 
 
 def tiles(a):
-    return functools.reduce(lambda p, r: p + r, [a[:, 128 * k : 128 * k + 128] for k in range(ROWS // 128)])
+    return functools.reduce(lambda p, r: p + r, [a[:, 128 * k : 128 * k + 128] for k in range(a.shape[1] // 128)])
 
 
 def kernel(
     src_h, tgt_h, slw_h, tlw_h, tim_h,
     rowp, moved, colp,
     src, tgt, own, far, slw, tlw, tim, sg, tg, mg, mv, tcat, scat, q, e, w, tw, eh, el,
-    r0, rb, rx1, rx2, qb, vr, vc, nb, sb, cb, part, frow, phi, f2, ff,
+    r0, rb, rx1, rx2, rd, qb, vr, vc, nb, sb, cb, part, frow, phi, f2, ff, fr, fc, half_t,
     send_sem, recv_sem, in_sem,
 ):
     me_s, me_t = lax.axis_index("src"), lax.axis_index("tgt")
@@ -49,6 +52,7 @@
     block = z // 2
     mate = z + 1 - 2 * (z % 2)
     opp = SIDE - 1 - z
+    mates_opp = SIDE - 1 - mate
     other = 1 - core
     mine = core == block
     started = []
@@ -83,8 +87,9 @@
     ]
     for load in loads:
         load.start()
+    stores = [pltpu.make_async_copy(a, b, in_sem.at[k]) for k, (a, b) in enumerate(((mv, moved), (fr, rowp), (fc, colp)))]
     barrier = pltpu.get_barrier_semaphore()
-    near = [dev(1), dev(-1), dev(dy=1), dev(dy=-1), dev(zz=mate), dev(zz=opp), dev(zz=opp, cc=other), dev(cc=other)]
+    near = [dev(1), dev(-1), dev(2), dev(dy=1), dev(dy=-1), dev(zz=mate), dev(zz=opp), dev(zz=opp, cc=other), dev(cc=other)]
     for device in near:
         pl.semaphore_signal(barrier, inc=1, device_id=device, device_id_type=MESH)
     for load in loads:
@@ -115,63 +120,50 @@
             ref = slot(self.buf, dx, zz, core, self.cols)
             self.c[key] = send(ref, ref, dev(zz=mate))
 
-        def round_x(self, key, zz):
+        def round_x(self, key, zz, shifts):
             ref = slot(self.buf, 0, zz, core, self.cols)
-            for d in (1, -1):
+            for d in shifts:
                 self.c[key, d] = send(ref, ref, dev(d))
 
-        def onward(self, key, zz):
-            for d in (1, -1):
-                self.c[key, d].wait_recv()
-                ref = slot(self.buf, -d, zz, core, chunk_half(self.n, d))
-                self.c[key, "f", d] = send(ref, ref, dev(d))
-
-        def end_of_round(self, key):
-            for d in (1, -1):
-                self.c[key, "f", d].wait_recv()
-
-        def start_near(self):
-            self.round_x("n", z)
+        def near(self):
+            self.round_x("n", z, (2, 1, -1))
             self.to_mate(("m", 0), 0, z)
             self.share(0, z)
 
-        def start_far(self):
+        def far(self):
             self.to_mate("fm", 0, opp)
-            self.round_x("f", opp)
             self.share(0, opp)
 
-        def step1(self):
-            self.onward("n", z)
-            for d in (1, -1):
+        def far_x(self):
+            self.round_x("f", opp, (1, -1))
+
+        def near_on(self):
+            for d in (1, -1, 2):
+                self.c["n", d].wait_recv()
                 self.to_mate(("m", -d), -d, z)
                 self.share(-d, z)
 
-        def step2(self):
+        def far_on(self):
             self.c["fm"].wait_recv()
-            self.round_x("g", SIDE - 1 - mate)
-            self.share(0, SIDE - 1 - mate)
-            self.onward("f", opp)
+            self.round_x("g", mates_opp, (2, 1, -1))
+            self.share(0, mates_opp)
             for d in (1, -1):
+                self.c["f", d].wait_recv()
+                ref = slot(self.buf, -d, opp, core, chunk_half(self.n, d))
+                self.c["ff", d] = send(ref, ref, dev(d))
                 self.share(-d, opp)
 
-        def step3(self):
-            self.end_of_round("n")
-            self.to_mate(("m", 2), 2, z)
-            self.share(2, z)
+        def last(self):
             self.c["m", 0].wait_recv()
             self.share(0, mate)
-            self.onward("g", SIDE - 1 - mate)
             for d in (1, -1):
-                self.share(-d, SIDE - 1 - mate)
-
-        def step4(self):
-            self.end_of_round("f")
+                self.c["ff", d].wait_recv()
             self.share(2, opp)
             for d in (1, -1, 2):
-                self.c["m", d].wait_recv()
-                self.share(d, mate)
-            self.end_of_round("g")
-            self.share(2, SIDE - 1 - mate)
+                self.c["m", -d].wait_recv()
+                self.share(-d, mate)
+                self.c["g", d].wait_recv()
+                self.share(-d, mates_opp)
 
         def finish(self):
             for copy in self.local:
@@ -238,27 +230,35 @@
         device_id=dev(zz=opp, cc=1), device_id_type=MESH,
     )
 
-    k_t = (number(), number())
-
-    def tslot(dy, cc, rows=None):
+    k_t = [(number(), number()) for _ in range(PARTS)]
+    parts = [pl.ds(k * PART, PART) for k in range(PARTS)]
+
+    def tslot(dy, cc, rows=None, cols=slice(None)):
         start, size = (0, 32) if rows is None else rows
-        return tg.at[pl.ds(pl.multiple_of(64 * wrap(y + dy) + 32 * cc + start, 16), size), :]
-
-    def tcopy(device, k):
+        return tg.at[pl.ds(pl.multiple_of(64 * wrap(y + dy) + 32 * cc + start, 16), size), cols]
+
+    def tcopy(device, k, which):
         return pltpu.make_async_remote_copy(
-            src_ref=tgt, dst_ref=tslot(0, core), send_sem=send_sem.at[k], recv_sem=recv_sem.at[k_t[0] + core],
+            src_ref=tgt.at[:, parts[k]], dst_ref=tslot(0, core, cols=parts[k]),
+            send_sem=send_sem.at[k_t[k][which]], recv_sem=recv_sem.at[k_t[k][0] + core],
             device_id=device, device_id_type=MESH,
         )
 
-    give_t = tcopy(dev(zz=opp, cc=1), k_t[0])
-    give_t_here = tcopy(dev(cc=0), k_t[1])
-    take_t = [copy_to(tgt, tslot(0, cc), dev(zz=opp, cc=1), k_t[cc]) for cc in (0, 1)]
-
-    give_t.start()
-
-    @pl.when(core == 1)
-    def _():
-        give_t_here.start()
+    give_t = [tcopy(dev(zz=opp, cc=1), k, 0) for k in range(PARTS)]
+    give_t_here = [tcopy(dev(cc=0), k, 1) for k in range(PARTS)]
+    take_t = [
+        [copy_to(tgt.at[:, parts[k]], tslot(0, cc, cols=parts[k]), dev(zz=opp, cc=1), k_t[k][cc]) for cc in (0, 1)]
+        for k in range(PARTS)
+    ]
+
+    def targets_out(k):
+        give_t[k].start()
+
+        @pl.when(core == 1)
+        def _():
+            give_t_here[k].start()
+
+    targets_out(0)
 
     @pl.when(mine)
     def _():
@@ -269,6 +269,8 @@
         give_far[0].start()
         give_far[1].start()
 
+    for k in range(1, PARTS):
+        targets_out(k)
     small = [
         send(own.at[0], far.at[0], dev(cc=other)),
         send(own.at[1], far.at[1], dev(cc=other)),
@@ -289,49 +291,63 @@
 
     gathers = [Gather(sg, n) for n in range(CHUNKS)]
     for g in gathers:
-        g.start_near()
-
-    @pl.when(core == 1)
-    def _():
-        take_t[0].wait_recv()
+        g.near()
 
     yc = {}
-    for cc in (0, 1):
-        if cc == 1:
-            take_t[1].wait_recv()
-        for d in (1, -1):
-            yc[cc, d] = send(tslot(0, cc), tslot(0, cc), dev(dy=d))
+
+    def targets_start(k):
+        for cc in (0, 1):
+            if cc == 0:
+
+                @pl.when(core == 1)
+                def _():
+                    take_t[k][0].wait_recv()
+            else:
+                take_t[k][1].wait_recv()
+            ref = tslot(0, cc, cols=parts[k])
+            for d in (1, -1):
+                yc[k, cc, d] = send(ref, ref, dev(dy=d))
+
+    targets_start(0)
     take_far.wait_recv()
     for g in gathers:
-        g.start_far()
-    gathers[0].step1()
-    for cc in (0, 1):
-        for d in (1, -1):
-            yc[cc, d].wait_recv()
-            ref = tslot(-d, cc, (0 if d == 1 else 16, 16))
-            yc[cc, "f", d] = send(ref, ref, dev(dy=d))
+        g.far()
+    for g in gathers:
+        g.far_x()
+
+    def targets_on(k):
+        for cc in (0, 1):
+            for d in (1, -1):
+                yc[k, cc, d].wait_recv()
+                ref = tslot(-d, cc, (0 if d == 1 else 16, 16), parts[k])
+                yc[k, cc, "f", d] = send(ref, ref, dev(dy=d))
+
+    def targets_in(k):
+        for cc in (0, 1):
+            for d in (1, -1):
+                yc[k, cc, "f", d].wait_recv()
+        cols = slice(k * PART, k * PART + PART)
+        half_t[:, cols] = 0.5 * jnp.sum(tg[:, cols] * tg[:, cols], axis=0, keepdims=True)
+        for b in range(k * PART // 128, (k + 1) * PART // 128):
+            here = slice(128 * b, 128 * b + 128)
+            high, low = halves(tg[:, here].T * SCALE)
+            tcat[here, 0:256] = high
+            tcat[here, 256:512] = high
+            tcat[here, 512:768] = low
+            cb[here, :] = jnp.broadcast_to(half_t[:, here] * SCALE, (128, 128)).T
+
+    gathers[0].near_on()
+    for k in range(1, PARTS):
+        targets_start(k)
     for g in gathers[1:]:
-        g.step1()
+        g.near_on()
+    targets_on(0)
     for g in gathers:
-        g.step2()
-    for g in gathers[:-1]:
-        g.step3()
-    for cc in (0, 1):
-        for d in (1, -1):
-            yc[cc, "f", d].wait_recv()
-
-    half_t = 0.5 * jnp.sum(tg[...] * tg[...], axis=0, keepdims=True)
-    for b in range(COLS // 128):
-        here = slice(128 * b, 128 * b + 128)
-        high, low = halves(tg[:, here].T * SCALE)
-        tcat[here, 0:256] = high
-        tcat[here, 256:512] = high
-        tcat[here, 512:768] = low
-    as_column(half_t * SCALE, cb)
-
-    gathers[-1].step3()
-    for g in gathers[:-1]:
-        g.step4()
+        g.far_on()
+    for k in range(1, PARTS):
+        targets_on(k)
+    gathers[0].last()
+    targets_in(0)
 
     def split_points(buf, n):
         cols = pl.ds(pl.multiple_of(n * WIDTH, WIDTH), WIDTH)
@@ -342,35 +358,65 @@
         scat[512:768, cols] = high
         return 0.5 * jnp.sum(a * a, axis=0, keepdims=True)
 
-    def cross_step(n, _):
-        cols = pl.ds(pl.multiple_of(n * WIDTH, WIDTH), WIDTH)
-        frow[:, cols] = split_points(sg, n)
-        cross = jnp.dot(tcat[...], scat[:, cols], preferred_element_type=F32)
-        bias = cb[...]
-        scores = cross - jnp.concatenate([bias, bias], axis=1)
-        q[:, cols] = scores
-        phi[:, cols] = jnp.max(scores, axis=0, keepdims=True)
-        return 0
-
-    def over_chunk(n, step):
+    def split_chunk(buf, n, norm):
+        def step(m, _):
+            cols = pl.ds(pl.multiple_of(m * WIDTH, WIDTH), WIDTH)
+            norm(cols, split_points(buf, m))
+            return 0
+
         lax.fori_loop(n * CHUNK // WIDTH, (n + 1) * CHUNK // WIDTH, step, 0)
 
-    for n, g in enumerate(gathers):
-        if n == CHUNKS - 1:
-            g.step4()
-        g.finish()
-        over_chunk(n, cross_step)
+    def blocks(n):
+        return [slice(k, k + BLOCK) for k in range(n * CHUNK, (n + 1) * CHUNK, BLOCK)]
+
+    def wide(a, pieces):
+        return jnp.concatenate([a] * pieces, axis=1)
+
+    def lane_top(a):
+        return functools.reduce(jnp.maximum, [a[:, k : k + 128] for k in range(0, a.shape[1], 128)])
+
+    def row_pass(body, first=0, size=COLS):
+        def step(r, acc):
+            return acc + body(pl.ds(pl.multiple_of(r * 8, 8), 8))
+
+        acc = lax.fori_loop(first // 8, (first + size) // 8, step, jnp.zeros((8, ROWS), F32), unroll=4)
+        return jnp.sum(acc, axis=0, keepdims=True)
+
+    row_lse = []
+    for k in range(PARTS):
+        here = slice(k * PART, k * PART + PART)
+        if k > 0:
+            targets_in(k)
+
+        for n, g in enumerate(gathers):
+            if k == 0:
+                if n > 0:
+                    g.last()
+                g.finish()
+
+                def norm(cols, value):
+                    frow[:, cols] = value
+
+                split_chunk(sg, n, norm)
+            for cols in blocks(n):
+                cross = jnp.dot(tcat[here, :], scat[:, cols], preferred_element_type=F32)
+                q[here, cols] = cross
+                phi[:, cols] = jnp.max(cross - wide(cb[here, :], BLOCK // 128), axis=0, keepdims=True)
+        top = phi[...]
+        row_lse.append(top + jnp.log(row_pass(lambda rows: jnp.exp2(q[rows, :] - wide(cb[rows, :], ROWS // 128) - top), k * PART, PART)) * LOG2E)
 
     arrived(small)
     slw[...] = jnp.where(mine, own[0], far[0])
     tim[...] = jnp.where(mine, own[1], far[1])
     tlw[...] = jnp.where(core == 0, own[2], far[2])[:, 0:COLS]
 
-    give_t.wait_send()
+    for k in range(PARTS):
+        give_t[k].wait_send()
 
     @pl.when(core == 1)
     def _():
-        give_t_here.wait_send()
+        for k in range(PARTS):
+            give_t_here[k].wait_send()
 
     @pl.when(mine)
     def _():
@@ -381,56 +427,51 @@
         give_far[0].wait_send()
         give_far[1].wait_send()
 
-    def row_pass(body):
-        def step(r, acc):
-            return acc + body(pl.ds(pl.multiple_of(r * 8, 8), 8))
-
-        acc = lax.fori_loop(0, COLS // 8, step, jnp.zeros((8, ROWS), F32), unroll=4)
-        return jnp.sum(acc, axis=0, keepdims=True)
-
-    top = phi[...]
-    total = row_pass(lambda rows: jnp.exp2(q[rows, :] - top))
-    copies = to_group(vr.at[0], top + jnp.log(total) * LOG2E)
+    copies = to_group(vr.at[0], lse_over_first(jnp.stack(row_lse)))
     arrived(copies)
     lse = lse_over_first(vr[0])
     phi[...] = slw[...] * LOG2E - lse
     frow[...] = frow[...] + EPSILON * (slw[...] - LN2 * lse)
 
-    def col_pass(keep):
-        def top_step(r, _):
-            rows = pl.ds(pl.multiple_of(r * 8, 8), 8)
-            scores = q[rows, :] + phi[...]
-            nb[rows, :] = functools.reduce(jnp.maximum, [scores[:, 128 * k : 128 * k + 128] for k in range(ROWS // 128)])
-            return 0
-
-        lax.fori_loop(0, COLS // 8, top_step, 0, unroll=4)
-
-        def join_step(r, _):
-            rows = pl.ds(pl.multiple_of(r * 128, 128), 128)
-            nb[rows, :] = jnp.broadcast_to(jnp.max(nb[rows, :], axis=1, keepdims=True), (128, 128))
-            return 0
-
-        lax.fori_loop(0, COLS // 128, join_step, 0)
-
-        def step(r, _):
-            rows = pl.ds(pl.multiple_of(r * 8, 8), 8)
-            p = jnp.exp2(q[rows, :] + phi[...] - jnp.concatenate([nb[rows, :]] * (ROWS // 128), axis=1))
-            if keep:
-                e[rows, :] = p
-            sb[rows, :] = tiles(p)
-            return 0
-
-        lax.fori_loop(0, COLS // 8, step, 0, unroll=4)
+    def join_tops():
+        for b in range(0, COLS, 128):
+            nb[b : b + 128, :] = jnp.broadcast_to(jnp.max(nb[b : b + 128, :], axis=1, keepdims=True), (128, 128))
+
+    def top_step(r, _):
+        rows = pl.ds(pl.multiple_of(r * 8, 8), 8)
+        nb[rows, :] = lane_top(q[rows, :] + phi[...])
+        return 0
+
+    def exp_step(r, _):
+        rows = pl.ds(pl.multiple_of(r * 8, 8), 8)
+        p = jnp.exp2(q[rows, :] + phi[...] - wide(nb[rows, :], ROWS // 128))
+        e[rows, :] = p
+        sb[rows, :] = tiles(p)
+        return 0
+
+    def column_lse():
         return column_top(nb), column_sum(sb)
 
-    ntop, total = col_pass(True)
+    lax.fori_loop(0, COLS // 8, top_step, 0, unroll=4)
+    join_tops()
+    lax.fori_loop(0, COLS // 8, exp_step, 0, unroll=4)
+    ntop, total = column_lse()
     copies = to_line(vc.at[0], ntop + jnp.log(total) * LOG2E)
+
+    def split_step(r, _):
+        rows = pl.ds(pl.multiple_of(r * 16, 16), 16)
+        high, low = halves(e[rows, :])
+        eh[rows, :] = high
+        el[rows, :] = low
+        return 0
+
+    lax.fori_loop(0, COLS // 16, split_step, 0, unroll=2)
     arrived(copies)
     factor = jnp.exp2(ntop + (tlw[...] * LOG2E - lse_over_first(vc[0])))
     as_column(factor, cb)
 
     def against_column(rows):
-        return e[rows, :] * jnp.concatenate([cb[rows, :]] * (ROWS // 128), axis=1)
+        return e[rows, :] * wide(cb[rows, :], ROWS // 128)
 
     copies = to_group(vr.at[1], row_pass(against_column))
     arrived(copies)
@@ -456,31 +497,21 @@
     high, low = halves(tg[...] * dual)
     tw[0:256, :] = high
     tw[256:512, :] = low
-    BLOCK = 512
-
     def wz(zz, cols, dx=None):
         return w.at[slice(None) if dx is None else wrap(x + dx), zz, core, :, cols]
 
-    mates_opp = SIDE - 1 - mate
     c = {}
-    for n in range(CHUNKS):
-        for m in range(n * CHUNK // BLOCK, (n + 1) * CHUNK // BLOCK):
-            cols = slice(m * BLOCK, m * BLOCK + BLOCK)
-
-            def split_step(r, _):
-                rows = pl.ds(pl.multiple_of(r * 16, 16), 16)
-                high, low = halves(e[rows, cols])
-                eh[rows, :] = high
-                el[rows, :] = low
-                return 0
-
-            lax.fori_loop(0, COLS // 16, split_step, 0, unroll=4)
-            acc = jnp.dot(tw[0:256, :], eh[...], preferred_element_type=F32)
-            acc = acc + jnp.dot(tw[0:256, :], el[...], preferred_element_type=F32)
-            acc = acc + jnp.dot(tw[256:512, :], eh[...], preferred_element_type=F32)
-            w[:, :, :, :, cols] = acc.reshape(SIDE, SIDE, 2, 8, BLOCK)
-        cols = chunk_cols(n)
-        c[n, "core"] = send(w.at[:, :, other, :, cols], r0.at[:, :, :, cols], dev(cc=other))
+
+    def weigh(m):
+        cols = slice(m * BLOCK, m * BLOCK + BLOCK)
+        acc = jnp.dot(tw[0:256, :], eh[:, cols], preferred_element_type=F32)
+        acc = acc + jnp.dot(tw[0:256, :], el[:, cols], preferred_element_type=F32)
+        acc = acc + jnp.dot(tw[256:512, :], eh[:, cols], preferred_element_type=F32)
+        w[:, :, :, :, cols] = acc.reshape(SIDE, SIDE, 2, 8, BLOCK)
+        n = m * BLOCK // CHUNK
+        if (m + 1) * BLOCK == (n + 1) * CHUNK:
+            cols = chunk_cols(n)
+            c[n, "core"] = send(w.at[:, :, other, :, cols], r0.at[:, :, :, cols], dev(cc=other))
 
     def rx_start(n, key, zz, k):
         for d in (1, -1):
@@ -501,30 +532,38 @@
         cols = chunk_cols(n)
         return wz(zz, cols, 0)[...] + rx2[k, 0, :, cols] + rx2[k, 1, :, cols]
 
+    def rx_direct(n, key, zz, k):
+        for i, d in enumerate((2, 1, -1)):
+            c[n, key, d] = send(wz(zz, chunk_cols(n), d), rd.at[k, i, :, chunk_cols(n)], dev(d))
+
+    def rx_sum(n, key, zz, k):
+        cols = chunk_cols(n)
+        for d in (1, -1, 2):
+            c[n, key, d].wait_recv()
+        return wz(zz, cols, 0)[...] + rd[k, 0, :, cols] + rd[k, 1, :, cols] + rd[k, 2, :, cols]
+
     def rs1(n):
         cols = chunk_cols(n)
         c[n, "core"].wait_recv()
         ref = w.at[:, :, core, :, cols]
         ref[...] = ref[...] + r0[:, :, :, cols]
         c[n, "mate"] = send(wz(mate, cols), rb.at[:, :, cols], dev(zz=mate))
-        rx_start(n, "m", mates_opp, 0)
-        rx_start(n, "o", opp, 1)
+        rx_direct(n, "m", mates_opp, 0)
+        rx_start(n, "o", opp, 0)
 
     def rs2(n):
         cols = chunk_cols(n)
-        rx_middle(n, "m", mates_opp, 0)
         c[n, "mate"].wait_recv()
         ref = wz(z, cols)
         ref[...] = ref[...] + rb[:, :, cols]
-        rx_start(n, "z", z, 2)
-        rx_middle(n, "o", opp, 1)
+        rx_direct(n, "z", z, 1)
+        rx_middle(n, "o", opp, 0)
 
     def rs3(n):
         cols = chunk_cols(n)
         qs = wz(mates_opp, cols, 0)
-        qs[...] = rx_end(n, "m", mates_opp, 0)
+        qs[...] = rx_sum(n, "m", mates_opp, 0)
         c[n, "last"] = send(qs, qb.at[:, cols], dev(zz=mate))
-        rx_middle(n, "z", z, 2)
 
     def point_rows(zz):
         return pl.ds(pl.multiple_of((x * SIDE + zz) * 16 + 8 * core, 8), 8)
@@ -538,13 +577,14 @@
         g = mgathers[n]
         ratio = tim[:, cols] / jnp.sum(vr[2, :, :, cols], axis=0)
         keep = 1.0 - tim[:, cols]
-        share = rx_end(n, "o", opp, 1)
+        share = rx_sum(n, "z", z, 1)
+        mg[point_rows(z), cols] = keep * sg[point_rows(z), cols] + ratio * share
+        g.near()
+        share = rx_end(n, "o", opp, 0)
         c[n, "last"].wait_recv()
         mg[point_rows(opp), cols] = keep * sg[point_rows(opp), cols] + ratio * (share + qb[:, cols])
-        g.start_far()
-        share = rx_end(n, "z", z, 2)
-        mg[point_rows(z), cols] = keep * sg[point_rows(z), cols] + ratio * share
-        g.start_near()
+        g.far()
+        g.far_x()
         here = mv.at[pl.ds(pl.multiple_of(8 * core, 8), 8), cols]
         there = mv.at[pl.ds(pl.multiple_of(8 * other, 8), 8), cols]
 
@@ -575,30 +615,73 @@
 
         outs.append((near_out, result_in(here, k_out[n][0] + core), result_in(there, k_out[n][0] + other)))
 
-    order = [rs1, rs2, rs3]
-    for stage in order:
-        for n in range(CHUNKS):
-            stage(n)
+    half = ROWS // BLOCK // 2
+    for m in range(half):
+        weigh(m)
+    weigh(half)
+    rs1(0)
+    for m in range(half + 1, 2 * half):
+        weigh(m)
+    rs2(0)
+    rs1(1)
+    rs3(0)
+    rs2(1)
     arrived(copies)
-    for n in range(CHUNKS):
-        rs4(n)
-
-    def last_step(n, _):
-        cols = pl.ds(pl.multiple_of(n * WIDTH, WIDTH), WIDTH)
-        phi[:, cols] = (f2[:, cols] - split_points(mg, n)) * SCALE
-        q[:, cols] = jnp.dot(tcat[...], scat[:, cols], preferred_element_type=F32)
-        return 0
-
-    for name in ("step1", "step2", "step3"):
-        for g in mgathers:
-            getattr(g, name)()
+    rs4(0)
+    rs3(1)
+    mgathers[0].near_on()
+    rs4(1)
+    mgathers[0].far_on()
+    mgathers[1].near_on()
+    mgathers[0].last()
+    mgathers[1].far_on()
+
+    def last_chunk(n):
+        def norm(cols, value):
+            phi[:, cols] = (f2[:, cols] - value) * SCALE
+
+        split_chunk(mg, n, norm)
+        for k, cols in enumerate(blocks(n)):
+            scores = jnp.dot(tcat[...], scat[:, cols], preferred_element_type=F32) + phi[:, cols]
+            q[:, cols] = scores
+            nb[...] = lane_top(scores) if k == 0 else jnp.maximum(nb[...], lane_top(scores))
+
+    def last_sums(n):
+        join_tops()
+
+        def step(r, _):
+            rows = pl.ds(pl.multiple_of(r * 8, 8), 8)
+            sb[rows, :] = tiles(jnp.exp2(q[rows, chunk_cols(n)] - wide(nb[rows, :], CHUNK // 128)))
+            return 0
+
+        lax.fori_loop(0, COLS // 8, step, 0, unroll=8)
+        ntop, total = column_lse()
+        return ntop + jnp.log(total) * LOG2E
+
+    def results():
+        for near_out, half_here, half_there in outs:
+            half_there.wait_recv()
+
+            @pl.when(jnp.logical_not(mine))
+            def _():
+                half_here.wait_recv()
+                near_out.wait_send()
+
+        fr[...] = jnp.where(mine, f2[...], ff[...])
+        for store in stores[:2]:
+            store.start()
+
+    col_lse = []
     for n, g in enumerate(mgathers):
-        g.step4()
         g.finish()
-        over_chunk(n, last_step)
-    ntop, total = col_pass(False)
+        last_chunk(n)
+        if n == 0:
+            results()
+        if n < CHUNKS - 1:
+            mgathers[n + 1].last()
+        col_lse.append(last_sums(n))
     home = z + core * (opp - z)
-    part[...] = ntop + jnp.log(total) * LOG2E - half_t * SCALE
+    part[...] = lse_over_first(jnp.stack(col_lse)) - half_t[...] * SCALE
 
     def to_owner(dy, cc, k, base):
         return pltpu.make_async_remote_copy(
@@ -633,18 +716,10 @@
 
     from_owner(more).wait_recv()
     arrived(waits)
-    colp[...] = EPSILON * (own[2][:, 0:COLS] - LN2 * lse_over_first(vc[2]))
-
-    rowp[...] = jnp.where(mine, f2[...], ff[...])
-    for near_out, half_here, half_there in outs:
-        half_there.wait_recv()
-
-        @pl.when(jnp.logical_not(mine))
-        def _():
-            half_here.wait_recv()
-            near_out.wait_send()
-
-    moved[...] = mv[...]
+    fc[...] = EPSILON * (own[2][:, 0:COLS] - LN2 * lse_over_first(vc[2]))
+    stores[2].start()
+    for store in stores:
+        store.wait()
 
     @pl.when(core == 1)
     def _():
@@ -655,7 +730,7 @@
 
 
 def per_device(sources, targets, source_logw, target_logw, times):
-    vmem, anywhere = pl.BlockSpec(memory_space=pltpu.VMEM), pl.BlockSpec(memory_space=pl.ANY)
+    anywhere = pl.BlockSpec(memory_space=pl.ANY)
     rowp, moved, colp = pl.pallas_call(
         kernel,
         out_shape=(
@@ -664,7 +739,7 @@
             jax.ShapeDtypeStruct((1, COLS), F32),
         ),
         in_specs=[anywhere] * 5,
-        out_specs=(vmem,) * 3,
+        out_specs=(anywhere,) * 3,
         scratch_shapes=[
             pltpu.VMEM((16, ROWS), F32),
             pltpu.VMEM((32, COLS), F32),
@@ -683,12 +758,13 @@
             pltpu.VMEM((COLS, ROWS), F32),
             pltpu.VMEM((SIDE, SIDE, 2, 8, ROWS), F32),
             pltpu.VMEM((2 * FEATURES, COLS), BF16),
-            pltpu.VMEM((COLS, 512), BF16),
-            pltpu.VMEM((COLS, 512), BF16),
+            pltpu.VMEM((COLS, ROWS), BF16),
+            pltpu.VMEM((COLS, ROWS), BF16),
             pltpu.VMEM((SIDE, SIDE, 8, ROWS), F32),
             pltpu.VMEM((SIDE, 8, ROWS), F32),
-            pltpu.VMEM((3, 8, ROWS), F32),
-            pltpu.VMEM((3, 2, 8, ROWS), F32),
+            pltpu.VMEM((1, 8, ROWS), F32),
+            pltpu.VMEM((1, 2, 8, ROWS), F32),
+            pltpu.VMEM((2, 3, 8, ROWS), F32),
             pltpu.VMEM((8, ROWS), F32),
             pltpu.VMEM((3, GROUP, 1, ROWS), F32),
             pltpu.VMEM((3, LINE, 1, COLS), F32),
@@ -700,6 +776,9 @@
             pltpu.VMEM((1, ROWS), F32),
             pltpu.VMEM((1, ROWS), F32),
             pltpu.VMEM((1, ROWS), F32),
+            pltpu.VMEM((1, ROWS), F32),
+            pltpu.VMEM((1, COLS), F32),
+            pltpu.VMEM((1, COLS), F32),
             pltpu.SemaphoreType.DMA((COPIES,)),
             pltpu.SemaphoreType.DMA((COPIES,)),
             pltpu.SemaphoreType.DMA((5,)),

time: 110 us -> 98.6 us (0.90)
  Pallas kernels: 106 us -> 94.3 us
    pallas_call x1, Pallas kernels: 106 us -> 94.3 us  [per_device(): pl.pallas_call(kernel, out_shape=(jax.ShapeDtypeStruct((1, ROWS), F32), j...]
where the time goes in v3:
time: 98.6 us; the launch traced here: 98.4 us
  Pallas kernels  94.3 us (96%)
  local copies, waits for them, and re-layouts  3.45 us (3%)
    pallas_call x1, Pallas kernels, per_device(): pl.pallas_call(kernel, out_shape=(jax.ShapeDtypeStruct((1, ROWS), F32), j...  94.3 us
    unnamed x7, local copies, waits for them, and re-layouts  3.45 us

profile of v3, /device:TPU:1, one launch (start us, length us, event | category | flops | bytes accessed | tf_op | source)
XLA Modules:
  0.0 98.4 jit_solution(17078933698230705659)
XLA Ops:
  0.6 94.3 %shard_map.76 = (f32[1,2048]{1,0:T(1,128)}, f32[16,2048]{1,0:T(8,128)}, f32[1,1024]{1,0:T(1,128)}) custom-call(f32[16,2048]{1,0:T(8,128)} %src_h.1, f32[32,1024]{1,0:T(8,128)} %tgt_h.1, f32[1,2048]{1,0:T(1,128)} %bitcast.5, f32[1,1024]{1,0:T(1,128)} %bitcast.8, f32[1,2048]{1,0:T(1,128)} %bitcast.6), custom_call_target="tpu_custom_call" | custom-call | tf_op jit(solution)/shard_map/pallas_call | solution.py:734
  95.0 0.0 copy-start
  95.0 0.7 copy-done
  95.7 0.6 copy.11
  96.3 0.0 copy-start.1
  96.3 1.6 %copy.12 = f32[16,2048]{1,0:T(8,128)} copy(f32[16,2048]{1,0:T(8,128)} %get-tuple-element.13) | data formatting | bytes 262144
  97.8 0.0 copy-done.1
  97.8 0.6 copy.13
Async XLA Ops:
  95.0 0.7 copy-start
  96.3 1.6 %copy-start.1 = (f32[1,1024]{1,0:T(1,128)S(1)}, f32[1,1024]{1,0:T(1,128)}, u32[]{:S(2)}) copy-start(f32[1,1024]{1,0:T(1,128)} %get-tuple-element.8) | copy-start | bytes 12292

commit v4 on v3

--- a/solution.py
+++ b/solution.py
@@ -21,9 +21,12 @@
 SIDE = 4
 GROUP = 16
 LINE = 8
-COPIES = 256
+ARRIVALS = 179
+DEPARTURES = 44
 CHUNKS = 2
 CHUNK = ROWS // CHUNKS
+PIECES = 4
+PIECE = ROWS // PIECES
 WIDTH = 256
 PARTS = 2
 PART = COLS // PARTS
@@ -63,23 +66,31 @@
     def dev(dx=0, dy=0, zz=z, cc=core):
         return (wrap(y + dy) * 2 + cc, wrap(x + dx) * SIDE + zz)
 
-    def copy_to(source, target, device, k):
+    def copy_to(source, target, device, k, out=0):
         return pltpu.make_async_remote_copy(
-            src_ref=source, dst_ref=target, send_sem=send_sem.at[k], recv_sem=recv_sem.at[k],
+            src_ref=source, dst_ref=target, send_sem=send_sem.at[out], recv_sem=recv_sem.at[k],
             device_id=device, device_id_type=MESH,
         )
 
-    count = [0]
+    count, leaves = [0], [0]
 
     def number():
         count[0] += 1
         return count[0] - 1
 
-    def send(source, target, device):
-        copy = copy_to(source, target, device, number())
+    def leave():
+        leaves[0] += 1
+        return leaves[0] - 1
+
+    def send(source, target, device, out=None, k=None):
+        copy = copy_to(source, target, device, number() if k is None else k, leave() if out is None else out)
         copy.start()
-        started.append(copy)
+        if out is None:
+            started.append(copy)
         return copy
+
+    def all_left(ref, out):
+        started.append(copy_to(ref, ref, dev(cc=other), 0, out))
 
     loads = [
         pltpu.make_async_copy(a, b, in_sem.at[k])
@@ -99,39 +110,41 @@
     def slot(buf, dx, zz, cc, cols):
         return buf.at[pl.ds(pl.multiple_of((wrap(x + dx) * SIDE + zz) * 16 + 8 * cc, 8), 8), cols]
 
-    def chunk_cols(n):
-        return pl.ds(n * CHUNK, CHUNK)
-
-    def chunk_half(n, d):
-        return pl.ds(n * CHUNK + (0 if d == 1 else CHUNK // 2), CHUNK // 2)
+    def chunk_cols(n, size=PIECE):
+        return pl.ds(n * size, size)
+
+    def chunk_half(n, d, size=PIECE):
+        return pl.ds(n * size + (0 if d == 1 else size // 2), size // 2)
 
     class Gather:
-        def __init__(self, buf, n):
-            self.buf, self.n = buf, n
-            self.cols = chunk_cols(n)
+        def __init__(self, buf, n, size):
+            self.buf, self.n, self.size = buf, n, size
+            self.cols = chunk_cols(n, size)
             self.c = {}
-            self.local = []
+            self.out, self.shared = leave(), number()
+            all_left(buf.at[0:240, self.cols], self.out)
 
         def share(self, dx, zz):
             ref = slot(self.buf, dx, zz, core, self.cols)
-            self.local.append(send(ref, ref, dev(cc=other)))
+            send(ref, ref, dev(cc=other), self.out, self.shared)
 
         def to_mate(self, key, dx, zz):
             ref = slot(self.buf, dx, zz, core, self.cols)
-            self.c[key] = send(ref, ref, dev(zz=mate))
+            self.c[key] = send(ref, ref, dev(zz=mate), self.out)
 
         def round_x(self, key, zz, shifts):
             ref = slot(self.buf, 0, zz, core, self.cols)
             for d in shifts:
-                self.c[key, d] = send(ref, ref, dev(d))
+                self.c[key, d] = send(ref, ref, dev(d), self.out)
 
         def near(self):
             self.round_x("n", z, (2, 1, -1))
             self.to_mate(("m", 0), 0, z)
             self.share(0, z)
 
-        def far(self):
-            self.to_mate("fm", 0, opp)
+        def far(self, pass_on=True):
+            if pass_on:
+                self.to_mate("fm", 0, opp)
             self.share(0, opp)
 
         def far_x(self):
@@ -143,14 +156,17 @@
                 self.to_mate(("m", -d), -d, z)
                 self.share(-d, z)
 
-        def far_on(self):
-            self.c["fm"].wait_recv()
+        def far_mate(self):
+            if "fm" in self.c:
+                self.c["fm"].wait_recv()
             self.round_x("g", mates_opp, (2, 1, -1))
             self.share(0, mates_opp)
+
+        def far_on(self):
             for d in (1, -1):
                 self.c["f", d].wait_recv()
-                ref = slot(self.buf, -d, opp, core, chunk_half(self.n, d))
-                self.c["ff", d] = send(ref, ref, dev(d))
+                ref = slot(self.buf, -d, opp, core, chunk_half(self.n, d, self.size))
+                self.c["ff", d] = send(ref, ref, dev(d), self.out)
                 self.share(-d, opp)
 
         def last(self):
@@ -166,8 +182,8 @@
                 self.share(-d, mates_opp)
 
         def finish(self):
-            for copy in self.local:
-                copy.wait_recv()
+            ref = self.buf.at[0:128, self.cols]
+            copy_to(ref, ref, dev(cc=other), self.shared).wait_recv()
 
     def group_devices():
         return [
@@ -183,7 +199,12 @@
 
     def to_all(buf, k, row, devices):
         buf[k] = row
-        return [send(buf.at[k], buf.at[k], device) for device in devices]
+        out, arrival = leave(), number()
+        for device in devices:
+            send(buf.at[k], buf.at[k], device, out, arrival)
+        whole = buf.at[0 : len(devices)]
+        all_left(whole, out)
+        return [copy_to(whole, whole, dev(cc=other), arrival)]
 
     def to_group(buf, row):
         return to_all(buf, group_slot, row, group_devices())
@@ -215,22 +236,19 @@
         )
 
     both = pl.ds(0, ROWS)
-    k_near = number()
-    k_far = (number(), number())
+    k_near, s_near = number(), leave()
+    k_far, s_far = number(), (leave(), leave())
 
     def out_half(cc):
         return src.at[pl.ds(pl.multiple_of(8 * cc, 8), 8), :]
 
-    give_near = copy_to(out_half(other), slot(sg, 0, z, other, both), dev(cc=other), k_near)
-    give_far = [copy_to(out_half(0), slot(sg, 0, z, 0, both), dev(zz=opp, cc=0), k_far[0]), None]
+    give_near = copy_to(out_half(other), slot(sg, 0, z, other, both), dev(cc=other), k_near, s_near)
+    give_far = [copy_to(out_half(cc), slot(sg, 0, z, cc, both), dev(zz=opp, cc=cc), k_far, s_far[cc]) for cc in (0, 1)]
     take_near = copy_to(out_half(0), slot(sg, 0, z, core, both), dev(cc=other), k_near)
-    take_far = copy_to(out_half(0), slot(sg, 0, opp, core, both), dev(zz=opp), k_far[0])
-    give_far[1] = pltpu.make_async_remote_copy(
-        src_ref=out_half(1), dst_ref=slot(sg, 0, z, 1, both), send_sem=send_sem.at[k_far[1]], recv_sem=recv_sem.at[k_far[0]],
-        device_id=dev(zz=opp, cc=1), device_id_type=MESH,
-    )
+    take_far = copy_to(out_half(0), slot(sg, 0, opp, core, both), dev(zz=opp), k_far)
 
     k_t = [(number(), number()) for _ in range(PARTS)]
+    s_t = [(leave(), leave()) for _ in range(PARTS)]
     parts = [pl.ds(k * PART, PART) for k in range(PARTS)]
 
     def tslot(dy, cc, rows=None, cols=slice(None)):
@@ -240,7 +258,7 @@
     def tcopy(device, k, which):
         return pltpu.make_async_remote_copy(
             src_ref=tgt.at[:, parts[k]], dst_ref=tslot(0, core, cols=parts[k]),
-            send_sem=send_sem.at[k_t[k][which]], recv_sem=recv_sem.at[k_t[k][0] + core],
+            send_sem=send_sem.at[s_t[k][which]], recv_sem=recv_sem.at[k_t[k][0] + core],
             device_id=device, device_id_type=MESH,
         )
 
@@ -289,11 +307,14 @@
     def _():
         take_near.wait_recv()
 
-    gathers = [Gather(sg, n) for n in range(CHUNKS)]
+    gathers = [Gather(sg, n, CHUNK) for n in range(CHUNKS)]
     for g in gathers:
         g.near()
 
     yc = {}
+    s_y = [leave() for _ in range(PARTS)]
+    for k in range(PARTS):
+        all_left(tg.at[0:192, parts[k]], s_y[k])
 
     def targets_start(k):
         for cc in (0, 1):
@@ -306,7 +327,7 @@
                 take_t[k][1].wait_recv()
             ref = tslot(0, cc, cols=parts[k])
             for d in (1, -1):
-                yc[k, cc, d] = send(ref, ref, dev(dy=d))
+                yc[k, cc, d] = send(ref, ref, dev(dy=d), s_y[k])
 
     targets_start(0)
     take_far.wait_recv()
@@ -320,7 +341,7 @@
             for d in (1, -1):
                 yc[k, cc, d].wait_recv()
                 ref = tslot(-d, cc, (0 if d == 1 else 16, 16), parts[k])
-                yc[k, cc, "f", d] = send(ref, ref, dev(dy=d))
+                yc[k, cc, "f", d] = send(ref, ref, dev(dy=d), s_y[k])
 
     def targets_in(k):
         for cc in (0, 1):
@@ -343,6 +364,7 @@
         g.near_on()
     targets_on(0)
     for g in gathers:
+        g.far_mate()
         g.far_on()
     for k in range(1, PARTS):
         targets_on(k)
@@ -358,16 +380,16 @@
         scat[512:768, cols] = high
         return 0.5 * jnp.sum(a * a, axis=0, keepdims=True)
 
-    def split_chunk(buf, n, norm):
+    def split_chunk(buf, n, size, norm):
         def step(m, _):
             cols = pl.ds(pl.multiple_of(m * WIDTH, WIDTH), WIDTH)
             norm(cols, split_points(buf, m))
             return 0
 
-        lax.fori_loop(n * CHUNK // WIDTH, (n + 1) * CHUNK // WIDTH, step, 0)
-
-    def blocks(n):
-        return [slice(k, k + BLOCK) for k in range(n * CHUNK, (n + 1) * CHUNK, BLOCK)]
+        lax.fori_loop(n * size // WIDTH, (n + 1) * size // WIDTH, step, 0)
+
+    def blocks(n, size):
+        return [slice(k, k + BLOCK) for k in range(n * size, (n + 1) * size, BLOCK)]
 
     def wide(a, pieces):
         return jnp.concatenate([a] * pieces, axis=1)
@@ -397,8 +419,8 @@
                 def norm(cols, value):
                     frow[:, cols] = value
 
-                split_chunk(sg, n, norm)
-            for cols in blocks(n):
+                split_chunk(sg, n, CHUNK, norm)
+            for cols in blocks(n, CHUNK):
                 cross = jnp.dot(tcat[here, :], scat[:, cols], preferred_element_type=F32)
                 q[here, cols] = cross
                 phi[:, cols] = jnp.max(cross - wide(cb[here, :], BLOCK // 128), axis=0, keepdims=True)
@@ -502,21 +524,22 @@
 
     c = {}
 
+    s_w = [leave() for _ in range(PIECES)]
+    for n in range(PIECES):
+        all_left(mg.at[0:240, chunk_cols(n)], s_w[n])
+
     def weigh(m):
-        cols = slice(m * BLOCK, m * BLOCK + BLOCK)
+        cols = slice(m * PIECE, m * PIECE + PIECE)
         acc = jnp.dot(tw[0:256, :], eh[:, cols], preferred_element_type=F32)
         acc = acc + jnp.dot(tw[0:256, :], el[:, cols], preferred_element_type=F32)
         acc = acc + jnp.dot(tw[256:512, :], eh[:, cols], preferred_element_type=F32)
-        w[:, :, :, :, cols] = acc.reshape(SIDE, SIDE, 2, 8, BLOCK)
-        n = m * BLOCK // CHUNK
-        if (m + 1) * BLOCK == (n + 1) * CHUNK:
-            cols = chunk_cols(n)
-            c[n, "core"] = send(w.at[:, :, other, :, cols], r0.at[:, :, :, cols], dev(cc=other))
+        w[:, :, :, :, cols] = acc.reshape(SIDE, SIDE, 2, 8, PIECE)
+        c[m, "core"] = send(w.at[:, :, other, :, cols], r0.at[:, :, :, cols], dev(cc=other), s_w[m])
 
     def rx_start(n, key, zz, k):
         for d in (1, -1):
             cut = chunk_half(n, d)
-            c[n, key, d] = send(wz(zz, cut, 2), rx1.at[k, :, cut], dev(d))
+            c[n, key, d] = send(wz(zz, cut, 2), rx1.at[k, :, cut], dev(d), s_w[n])
 
     def rx_middle(n, key, zz, k):
         for d in (1, -1):
@@ -524,7 +547,7 @@
             c[n, key, d].wait_recv()
             ref = wz(zz, cut, d)
             ref[...] = ref[...] + rx1[k, :, cut]
-            c[n, key, "s", d] = send(wz(zz, chunk_cols(n), d), rx2.at[k, 0 if d == 1 else 1, :, chunk_cols(n)], dev(d))
+            c[n, key, "s", d] = send(wz(zz, chunk_cols(n), d), rx2.at[k, 0 if d == 1 else 1, :, chunk_cols(n)], dev(d), s_w[n])
 
     def rx_end(n, key, zz, k):
         for d in (1, -1):
@@ -533,13 +556,14 @@
         return wz(zz, cols, 0)[...] + rx2[k, 0, :, cols] + rx2[k, 1, :, cols]
 
     def rx_direct(n, key, zz, k):
+        c[n, key] = number()
         for i, d in enumerate((2, 1, -1)):
-            c[n, key, d] = send(wz(zz, chunk_cols(n), d), rd.at[k, i, :, chunk_cols(n)], dev(d))
+            send(wz(zz, chunk_cols(n), d), rd.at[k, i, :, chunk_cols(n)], dev(d), s_w[n], c[n, key])
 
     def rx_sum(n, key, zz, k):
         cols = chunk_cols(n)
-        for d in (1, -1, 2):
-            c[n, key, d].wait_recv()
+        ref = rd.at[k, :, :, cols]
+        copy_to(ref, ref, dev(1), c[n, key]).wait_recv()
         return wz(zz, cols, 0)[...] + rd[k, 0, :, cols] + rd[k, 1, :, cols] + rd[k, 2, :, cols]
 
     def rs1(n):
@@ -547,7 +571,7 @@
         c[n, "core"].wait_recv()
         ref = w.at[:, :, core, :, cols]
         ref[...] = ref[...] + r0[:, :, :, cols]
-        c[n, "mate"] = send(wz(mate, cols), rb.at[:, :, cols], dev(zz=mate))
+        c[n, "mate"] = send(wz(mate, cols), rb.at[:, :, cols], dev(zz=mate), s_w[n])
         rx_direct(n, "m", mates_opp, 0)
         rx_start(n, "o", opp, 0)
 
@@ -563,13 +587,14 @@
         cols = chunk_cols(n)
         qs = wz(mates_opp, cols, 0)
         qs[...] = rx_sum(n, "m", mates_opp, 0)
-        c[n, "last"] = send(qs, qb.at[:, cols], dev(zz=mate))
+        c[n, "last"] = send(qs, qb.at[:, cols], dev(zz=mate), s_w[n])
 
     def point_rows(zz):
         return pl.ds(pl.multiple_of((x * SIDE + zz) * 16 + 8 * core, 8), 8)
 
-    mgathers = [Gather(mg, n) for n in range(CHUNKS)]
-    k_out = [(number(), number()) for _ in range(CHUNKS)]
+    mgathers = [Gather(mg, n, PIECE) for n in range(PIECES)]
+    k_out = [(number(), number()) for _ in range(PIECES)]
+    s_out = [(leave(), leave()) for _ in range(PIECES)]
     outs = []
 
     def rs4(n):
@@ -594,8 +619,8 @@
                 device_id=device, device_id_type=MESH,
             )
 
-        far_out = result(opp, dev(zz=opp, cc=block), k_out[n][0])
-        near_out = result(z, dev(cc=other), k_out[n][1])
+        far_out = result(opp, dev(zz=opp, cc=block), s_out[n][0])
+        near_out = result(z, dev(cc=other), s_out[n][1])
         far_out.start()
         started.append(far_out)
 
@@ -609,52 +634,70 @@
 
         def result_in(ref, k):
             return pltpu.make_async_remote_copy(
-                src_ref=ref, dst_ref=ref, send_sem=send_sem.at[k_out[n][0]], recv_sem=recv_sem.at[k],
+                src_ref=ref, dst_ref=ref, send_sem=send_sem.at[s_out[n][0]], recv_sem=recv_sem.at[k],
                 device_id=dev(cc=other), device_id_type=MESH,
             )
 
         outs.append((near_out, result_in(here, k_out[n][0] + core), result_in(there, k_out[n][0] + other)))
 
-    half = ROWS // BLOCK // 2
-    for m in range(half):
-        weigh(m)
-    weigh(half)
+    def gather_on(n):
+        mgathers[n].near_on()
+        mgathers[n].far_mate()
+        mgathers[n].far_on()
+
+    weigh(0)
+    weigh(1)
     rs1(0)
-    for m in range(half + 1, 2 * half):
-        weigh(m)
+    weigh(2)
+    rs1(1)
+    weigh(3)
     rs2(0)
-    rs1(1)
     rs3(0)
+    rs1(2)
     rs2(1)
+    rs3(1)
+    rs1(3)
     arrived(copies)
     rs4(0)
-    rs3(1)
-    mgathers[0].near_on()
+    rs2(2)
+    rs3(2)
     rs4(1)
-    mgathers[0].far_on()
-    mgathers[1].near_on()
+    gather_on(0)
+    rs2(3)
+    rs3(3)
+    rs4(2)
+    gather_on(1)
+    rs4(3)
     mgathers[0].last()
-    mgathers[1].far_on()
+    gather_on(2)
 
     def last_chunk(n):
         def norm(cols, value):
             phi[:, cols] = (f2[:, cols] - value) * SCALE
 
-        split_chunk(mg, n, norm)
-        for k, cols in enumerate(blocks(n)):
-            scores = jnp.dot(tcat[...], scat[:, cols], preferred_element_type=F32) + phi[:, cols]
-            q[:, cols] = scores
-            nb[...] = lane_top(scores) if k == 0 else jnp.maximum(nb[...], lane_top(scores))
-
-    def last_sums(n):
-        join_tops()
+        split_chunk(mg, n, PIECE, norm)
+        cols = slice(n * PIECE, n * PIECE + PIECE)
+        scores = jnp.dot(tcat[...], scat[:, cols], preferred_element_type=F32) + phi[:, cols]
+        q[:, cols] = scores
+        if n == 0:
+            nb[...] = lane_top(scores)
+        else:
+            fresh = jnp.maximum(nb[...], lane_top(scores))
+            sb[...] = sb[...] * jnp.exp2(nb[...] - fresh)
+            nb[...] = fresh
 
         def step(r, _):
             rows = pl.ds(pl.multiple_of(r * 8, 8), 8)
-            sb[rows, :] = tiles(jnp.exp2(q[rows, chunk_cols(n)] - wide(nb[rows, :], CHUNK // 128)))
+            part_sum = tiles(jnp.exp2(q[rows, cols] - wide(nb[rows, :], PIECE // 128)))
+            sb[rows, :] = part_sum if n == 0 else sb[rows, :] + part_sum
             return 0
 
         lax.fori_loop(0, COLS // 8, step, 0, unroll=8)
+
+    def last_lse():
+        cb[...] = nb[...]
+        join_tops()
+        sb[...] = sb[...] * jnp.exp2(cb[...] - nb[...])
         ntop, total = column_lse()
         return ntop + jnp.log(total) * LOG2E
 
@@ -671,17 +714,22 @@
         for store in stores[:2]:
             store.start()
 
-    col_lse = []
-    for n, g in enumerate(mgathers):
-        g.finish()
-        last_chunk(n)
-        if n == 0:
-            results()
-        if n < CHUNKS - 1:
-            mgathers[n + 1].last()
-        col_lse.append(last_sums(n))
+    mgathers[0].finish()
+    last_chunk(0)
+    results()
+    mgathers[1].last()
+    gather_on(3)
+    mgathers[1].finish()
+    last_chunk(1)
+    mgathers[2].last()
+    mgathers[2].finish()
+    last_chunk(2)
+    mgathers[3].last()
+    mgathers[3].finish()
+    last_chunk(3)
+
     home = z + core * (opp - z)
-    part[...] = lse_over_first(jnp.stack(col_lse)) - half_t[...] * SCALE
+    part[...] = last_lse() - half_t[...] * SCALE
 
     def to_owner(dy, cc, k, base):
         return pltpu.make_async_remote_copy(
@@ -695,13 +743,13 @@
     waits = []
     for dy in (2, 1, -1):
         base, more = number(), number()
-        for cc, k in ((0, base), (1, more)):
-            copy = to_owner(dy, cc, k, base)
+        for cc in (0, 1):
+            copy = to_owner(dy, cc, leave(), base)
             copy.start()
             started.append(copy)
         waits += [from_owner(base), from_owner(more)]
     base, more = number(), number()
-    to_one, to_zero = to_owner(0, 1, more, base), to_owner(0, 0, base, base)
+    to_one, to_zero = to_owner(0, 1, leave(), base), to_owner(0, 0, leave(), base)
     to_one.start()
     started.append(to_one)
 
@@ -779,8 +827,8 @@
             pltpu.VMEM((1, ROWS), F32),
             pltpu.VMEM((1, COLS), F32),
             pltpu.VMEM((1, COLS), F32),
-            pltpu.SemaphoreType.DMA((COPIES,)),
-            pltpu.SemaphoreType.DMA((COPIES,)),
+            pltpu.SemaphoreType.DMA((DEPARTURES,)),
+            pltpu.SemaphoreType.DMA((ARRIVALS,)),
             pltpu.SemaphoreType.DMA((5,)),
         ],
         compiler_params=pltpu.CompilerParams(

time: 98.6 us -> 93 us (0.943)
  Pallas kernels: 94.3 us -> 88.8 us
    pallas_call x1, Pallas kernels: 94.3 us -> 88.8 us  [per_device(): pl.pallas_call(kernel, out_shape=(jax.ShapeDtypeStruct((1, ROWS), F32), j...]
where the time goes in v4:
time: 93 us; the launch traced here: 92.9 us
  Pallas kernels  88.8 us (95%)
  local copies, waits for them, and re-layouts  3.45 us (4%)
    pallas_call x1, Pallas kernels, per_device(): pl.pallas_call(kernel, out_shape=(jax.ShapeDtypeStruct((1, ROWS), F32), j...  88.8 us
    unnamed x7, local copies, waits for them, and re-layouts  3.45 us

profile of v4, /device:TPU:1, one launch (start us, length us, event | category | flops | bytes accessed | tf_op | source)
XLA Modules:
  0.0 92.9 jit_solution(4251822015369969171)
XLA Ops:
  0.6 88.8 %shard_map.76 = (f32[1,2048]{1,0:T(1,128)}, f32[16,2048]{1,0:T(8,128)}, f32[1,1024]{1,0:T(1,128)}) custom-call(f32[16,2048]{1,0:T(8,128)} %src_h.1, f32[32,1024]{1,0:T(8,128)} %tgt_h.1, f32[1,2048]{1,0:T(1,128)} %bitcast.5, f32[1,1024]{1,0:T(1,128)} %bitcast.8, f32[1,2048]{1,0:T(1,128)} %bitcast.6), custom_call_target="tpu_custom_call" | custom-call | tf_op jit(solution)/shard_map/pallas_call | solution.py:782
  89.4 0.0 copy-start
  89.4 0.7 copy-done
  90.1 0.6 copy.11
  90.7 0.0 copy-start.1
  90.7 1.6 %copy.12 = f32[16,2048]{1,0:T(8,128)} copy(f32[16,2048]{1,0:T(8,128)} %get-tuple-element.13) | data formatting | bytes 262144
  92.3 0.0 copy-done.1
  92.3 0.6 copy.13
Async XLA Ops:
  89.4 0.7 copy-start
  90.7 1.6 %copy-start.1 = (f32[1,1024]{1,0:T(1,128)S(1)}, f32[1,1024]{1,0:T(1,128)}, u32[]{:S(2)}) copy-start(f32[1,1024]{1,0:T(1,128)} %get-tuple-element.8) | copy-start | bytes 12292

commit v5 on v4

--- a/solution.py
+++ b/solution.py
@@ -21,7 +21,7 @@
 SIDE = 4
 GROUP = 16
 LINE = 8
-ARRIVALS = 179
+ARRIVALS = 143
 DEPARTURES = 44
 CHUNKS = 2
 CHUNK = ROWS // CHUNKS
@@ -122,20 +122,21 @@
             self.cols = chunk_cols(n, size)
             self.c = {}
             self.out, self.shared = leave(), number()
+            self.from_mate, self.second, self.third = number(), number(), number()
             all_left(buf.at[0:240, self.cols], self.out)
 
         def share(self, dx, zz):
             ref = slot(self.buf, dx, zz, core, self.cols)
             send(ref, ref, dev(cc=other), self.out, self.shared)
 
-        def to_mate(self, key, dx, zz):
+        def to_mate(self, key, dx, zz, k=None):
             ref = slot(self.buf, dx, zz, core, self.cols)
-            self.c[key] = send(ref, ref, dev(zz=mate), self.out)
-
-        def round_x(self, key, zz, shifts):
+            self.c[key] = send(ref, ref, dev(zz=mate), self.out, k)
+
+        def round_x(self, key, zz, shifts, k=None):
             ref = slot(self.buf, 0, zz, core, self.cols)
             for d in shifts:
-                self.c[key, d] = send(ref, ref, dev(d), self.out)
+                self.c[key, d] = send(ref, ref, dev(d), self.out, k)
 
         def near(self):
             self.round_x("n", z, (2, 1, -1))
@@ -153,37 +154,40 @@
         def near_on(self):
             for d in (1, -1, 2):
                 self.c["n", d].wait_recv()
-                self.to_mate(("m", -d), -d, z)
+                self.to_mate(("m", -d), -d, z, self.from_mate)
                 self.share(-d, z)
 
         def far_mate(self):
             if "fm" in self.c:
                 self.c["fm"].wait_recv()
-            self.round_x("g", mates_opp, (2, 1, -1))
+            self.round_x("g", mates_opp, (2, 1, -1), self.third)
             self.share(0, mates_opp)
 
         def far_on(self):
             for d in (1, -1):
                 self.c["f", d].wait_recv()
                 ref = slot(self.buf, -d, opp, core, chunk_half(self.n, d, self.size))
-                self.c["ff", d] = send(ref, ref, dev(d), self.out)
+                send(ref, ref, dev(d), self.out, self.second)
                 self.share(-d, opp)
 
         def last(self):
             self.c["m", 0].wait_recv()
             self.share(0, mate)
-            for d in (1, -1):
-                self.c["ff", d].wait_recv()
+            self.rows_in(8, self.second)
             self.share(2, opp)
-            for d in (1, -1, 2):
-                self.c["m", -d].wait_recv()
-                self.share(-d, mate)
-                self.c["g", d].wait_recv()
-                self.share(-d, mates_opp)
+            self.rows_in(24, self.from_mate)
+            for dx in (1, -1, 2):
+                self.share(dx, mate)
+            self.rows_in(24, self.third)
+            for dx in (1, -1, 2):
+                self.share(dx, mates_opp)
+
+        def rows_in(self, rows, k):
+            ref = self.buf.at[0:rows, self.cols]
+            copy_to(ref, ref, dev(cc=other), k).wait_recv()
 
         def finish(self):
-            ref = self.buf.at[0:128, self.cols]
-            copy_to(ref, ref, dev(cc=other), self.shared).wait_recv()
+            self.rows_in(128, self.shared)
 
     def group_devices():
         return [
@@ -316,6 +320,8 @@
     for k in range(PARTS):
         all_left(tg.at[0:192, parts[k]], s_y[k])
 
+    k_f = [number() for _ in range(PARTS)]
+
     def targets_start(k):
         for cc in (0, 1):
             if cc == 0:
@@ -341,12 +347,11 @@
             for d in (1, -1):
                 yc[k, cc, d].wait_recv()
                 ref = tslot(-d, cc, (0 if d == 1 else 16, 16), parts[k])
-                yc[k, cc, "f", d] = send(ref, ref, dev(dy=d), s_y[k])
+                send(ref, ref, dev(dy=d), s_y[k], k_f[k])
 
     def targets_in(k):
-        for cc in (0, 1):
-            for d in (1, -1):
-                yc[k, cc, "f", d].wait_recv()
+        ref = tg.at[0:64, parts[k]]
+        copy_to(ref, ref, dev(dy=1), k_f[k]).wait_recv()
         cols = slice(k * PART, k * PART + PART)
         half_t[:, cols] = 0.5 * jnp.sum(tg[:, cols] * tg[:, cols], axis=0, keepdims=True)
         for b in range(k * PART // 128, (k + 1) * PART // 128):
@@ -511,11 +516,9 @@
     copies = to_line(vc.at[1], factor * column_sum(sb))
     arrived(copies)
     dual = factor * (jnp.exp(tlw[...]) / jnp.sum(vc[1], axis=0))
-    as_column(dual, cb)
 
     potential.wait_recv()
 
-    copies = to_group(vr.at[2], row_pass(against_column))
     high, low = halves(tg[...] * dual)
     tw[0:256, :] = high
     tw[256:512, :] = low
@@ -648,6 +651,8 @@
     weigh(0)
     weigh(1)
     rs1(0)
+    as_column(dual, cb)
+    copies = to_group(vr.at[2], row_pass(against_column))
     weigh(2)
     rs1(1)
     weigh(3)

time: 93 us -> 92.5 us (level)
  no operation moved by 1% of the time
where the time goes in v5:
time: 92.5 us; the launch traced here: 92.4 us
  Pallas kernels  88.3 us (95%)
  local copies, waits for them, and re-layouts  3.45 us (4%)
    pallas_call x1, Pallas kernels, per_device(): pl.pallas_call(kernel, out_shape=(jax.ShapeDtypeStruct((1, ROWS), F32), j...  88.3 us
    unnamed x7, local copies, waits for them, and re-layouts  3.45 us

profile of v5, /device:TPU:1, one launch (start us, length us, event | category | flops | bytes accessed | tf_op | source)
XLA Modules:
  0.0 92.4 jit_solution(16990461485770969589)
XLA Ops:
  0.6 88.3 %shard_map.76 = (f32[1,2048]{1,0:T(1,128)}, f32[16,2048]{1,0:T(8,128)}, f32[1,1024]{1,0:T(1,128)}) custom-call(f32[16,2048]{1,0:T(8,128)} %src_h.1, f32[32,1024]{1,0:T(8,128)} %tgt_h.1, f32[1,2048]{1,0:T(1,128)} %bitcast.5, f32[1,1024]{1,0:T(1,128)} %bitcast.8, f32[1,2048]{1,0:T(1,128)} %bitcast.6), custom_call_target="tpu_custom_call" | custom-call | tf_op jit(solution)/shard_map/pallas_call | solution.py:787
  88.9 0.0 copy-start
  88.9 0.7 copy-done
  89.6 0.6 copy.11
  90.2 0.0 copy-start.1
  90.2 1.6 %copy.12 = f32[16,2048]{1,0:T(8,128)} copy(f32[16,2048]{1,0:T(8,128)} %get-tuple-element.13) | data formatting | bytes 262144
  91.8 0.0 copy-done.1
  91.8 0.6 copy.13
Async XLA Ops:
  88.9 0.7 copy-start
  90.2 1.6 %copy-start.1 = (f32[1,1024]{1,0:T(1,128)S(1)}, f32[1,1024]{1,0:T(1,128)}, u32[]{:S(2)}) copy-start(f32[1,1024]{1,0:T(1,128)} %get-tuple-element.8) | copy-start | bytes 12292

commit v6 on v5

--- a/solution.py
+++ b/solution.py
@@ -406,7 +406,7 @@
         def step(r, acc):
             return acc + body(pl.ds(pl.multiple_of(r * 8, 8), 8))
 
-        acc = lax.fori_loop(first // 8, (first + size) // 8, step, jnp.zeros((8, ROWS), F32), unroll=4)
+        acc = lax.fori_loop(first // 8, (first + size) // 8, step, jnp.zeros((8, ROWS), F32), unroll=8)
         return jnp.sum(acc, axis=0, keepdims=True)
 
     row_lse = []
@@ -479,7 +479,7 @@
     def column_lse():
         return column_top(nb), column_sum(sb)
 
-    lax.fori_loop(0, COLS // 8, top_step, 0, unroll=4)
+    lax.fori_loop(0, COLS // 8, top_step, 0, unroll=8)
     join_tops()
     lax.fori_loop(0, COLS // 8, exp_step, 0, unroll=4)
     ntop, total = column_lse()
@@ -512,7 +512,7 @@
         sb[rows, :] = tiles(e[rows, :] * phi[...])
         return 0
 
-    lax.fori_loop(0, COLS // 8, weigh_step, 0, unroll=4)
+    lax.fori_loop(0, COLS // 8, weigh_step, 0, unroll=8)
     copies = to_line(vc.at[1], factor * column_sum(sb))
     arrived(copies)
     dual = factor * (jnp.exp(tlw[...]) / jnp.sum(vc[1], axis=0))

time: 92.5 us -> 91.8 us (level)
  no operation moved by 1% of the time
where the time goes in v6:
time: 91.8 us; the launch traced here: 91.6 us
  Pallas kernels  87.5 us (95%)
  local copies, waits for them, and re-layouts  3.45 us (4%)
    pallas_call x1, Pallas kernels, per_device(): pl.pallas_call(kernel, out_shape=(jax.ShapeDtypeStruct((1, ROWS), F32), j...  87.5 us
    unnamed x7, local copies, waits for them, and re-layouts  3.45 us

profile of v6, /device:TPU:1, one launch (start us, length us, event | category | flops | bytes accessed | tf_op | source)
XLA Modules:
  0.0 91.6 jit_solution(14121531573106761825)
XLA Ops:
  0.6 87.5 %shard_map.76 = (f32[1,2048]{1,0:T(1,128)}, f32[16,2048]{1,0:T(8,128)}, f32[1,1024]{1,0:T(1,128)}) custom-call(f32[16,2048]{1,0:T(8,128)} %src_h.1, f32[32,1024]{1,0:T(8,128)} %tgt_h.1, f32[1,2048]{1,0:T(1,128)} %bitcast.5, f32[1,1024]{1,0:T(1,128)} %bitcast.8, f32[1,2048]{1,0:T(1,128)} %bitcast.6), custom_call_target="tpu_custom_call" | custom-call | tf_op jit(solution)/shard_map/pallas_call | solution.py:787
  88.1 0.0 copy-start
  88.1 0.7 copy-done
  88.8 0.6 copy.11
  89.4 0.0 copy-start.1
  89.4 1.6 %copy.12 = f32[16,2048]{1,0:T(8,128)} copy(f32[16,2048]{1,0:T(8,128)} %get-tuple-element.13) | data formatting | bytes 262144
  91.0 0.0 copy-done.1
  91.0 0.6 copy.13
Async XLA Ops:
  88.1 0.7 copy-start
  89.4 1.6 %copy-start.1 = (f32[1,1024]{1,0:T(1,128)S(1)}, f32[1,1024]{1,0:T(1,128)}, u32[]{:S(2)}) copy-start(f32[1,1024]{1,0:T(1,128)} %get-tuple-element.8) | copy-start | bytes 12292
